TPU v7x, 32 devices: a whole 2x2x4 slice. The times are simulated.
32 devices in a mesh: space: 4 (over y, x), mom: 8 (over z, core).
Axes of the slice: x: 2, y: 2, z: 4, core: 2. Of those that a mesh axis runs over, the one named last changes fastest.
Arguments:
- density: float32 [256, 256, 512], P('mom', None, 'space'), may hold values from -6 to 6
- mode_waves: int32 [16, 2], replicated, may hold values from -7 to 7
- mode_amplitudes: float32 [16], replicated, may hold values from -3 to 3
- mode_phases: float32 [16], replicated, may hold values from -3.140625 to 3.140625
Outputs:
- time_rate: float32 [256, 256, 512], P('mom', None, 'space')
All inputs are finite; a program needn't handle non-finite values.
Results may differ from a plain program's by a relative error of at most 0.0003.
Values sent between devices are 32-bit elements; how exact they have to be, the bound alone decides.
A program may use at most 128 MiB of HBM per device.

v0:
```python
import math

import jax
import jax.numpy as jnp
from jax import lax
from jax.sharding import PartitionSpec as P

NY = 16


HIGHEST_PRECISION = lax.Precision.HIGHEST
DAMPING = 0.5
FRICTION = 0.5


def extended(value, sides, width):
    for axis, dim in sides:
        peers, length = (lax.axis_size(axis), value.shape[dim])
        up = [(i, (i + 1) % peers) for i in range(peers)]
        down = [(j, i) for i, j in up]
        last = lax.slice_in_dim(value, length - width, length, axis=dim)
        leading = lax.slice_in_dim(value, 0, width, axis=dim)
        before = lax.ppermute(last, axis, up)
        after = lax.ppermute(leading, axis, down)
        value = jnp.concatenate([before, value, after], axis=dim)
    return value


def velocity(indices, points):
    return (2 * indices - points + 1).astype(jnp.float32) / points


def signed_frequency(indices, points):
    return jnp.where(indices < points // 2, indices, indices - points)


def fourier_tables(points):
    indices = jnp.arange(points, dtype=jnp.int32)
    turned = indices[:, None] * indices[None, :] % points
    angles = 2.0 * math.pi / points * turned.astype(jnp.float32)
    return (jnp.cos(angles), jnp.sin(angles))


def cell_factors(
    mode_waves, mode_amplitudes, mode_phases, row_number, column_number, total_rows, total_columns
):
    turn_rows = mode_waves[:, 0:1] * row_number[None, :] % total_rows
    turn_columns = mode_waves[:, 1:2] * column_number[None, :] % total_columns
    angles = (
        2.0
        * math.pi
        * (
            turn_rows.astype(jnp.float32) / total_rows
            + turn_columns.astype(jnp.float32) / total_columns
        )
        + mode_phases[:, None]
    )
    return mode_amplitudes[:, None] * jnp.sin(angles)


def freq_factors(mode_waves, first_freq, second_freq, points):
    summed = (
        mode_waves[None, None, :, 0] * first_freq[:, None, None]
        + mode_waves[None, None, :, 1] * second_freq[None, :, None]
    ) % (2 * points)
    values = jnp.sin(math.pi / points * summed.astype(jnp.float32))
    return values.reshape(first_freq.shape[0] * second_freq.shape[0], mode_waves.shape[0])


def damping_table(first_freq, second_freq, points):
    squares = (
        first_freq[:, None] * first_freq[:, None] + second_freq[None, :] * second_freq[None, :]
    )
    return DAMPING / (points // 2 * (points // 2)) * squares.astype(jnp.float32)


def planes_first(operand, matrix):
    return jnp.einsum("ckb,km->cmb", operand, matrix, precision=HIGHEST_PRECISION)


def planes_second(operand, matrix):
    return jnp.einsum("cak,km->cam", operand, matrix, precision=HIGHEST_PRECISION)


def upwind(shifted):
    minus_side = (
        -2.0 * shifted(-3)
        + 15.0 * shifted(-2)
        - 60.0 * shifted(-1)
        + 20.0 * shifted(0)
        + 30.0 * shifted(1)
        - 3.0 * shifted(2)
    ) / 60.0
    plus_side = (
        2.0 * shifted(3)
        - 15.0 * shifted(2)
        + 60.0 * shifted(1)
        - 20.0 * shifted(0)
        - 30.0 * shifted(-1)
        + 3.0 * shifted(-2)
    ) / 60.0
    return (minus_side, plus_side)


def advect(density, row_speeds, column_speeds):
    plane_rows, points, cell_dev = density.shape
    rows_dev = cell_dev // NY
    padded = extended(density, (("space", 2),), 3 * NY)

    def across(offset):
        first_cell = (3 + offset) * NY
        return padded[:, :, first_cell : first_cell + cell_dev]

    cell_grid = density.reshape(plane_rows, points, rows_dev, NY)

    def along_row(offset):
        return jnp.roll(cell_grid, -offset, axis=3).reshape(plane_rows, points, cell_dev)

    minus_rows, plus_rows = upwind(across)
    minus_columns, plus_columns = upwind(along_row)
    speed_rows = row_speeds[:, None, None]
    speed_columns = column_speeds[None, :, None]
    return speed_rows * jnp.where(
        speed_rows > 0, minus_rows, plus_rows
    ) + speed_columns * jnp.where(speed_columns > 0, minus_columns, plus_columns)


def transform_planes(planes, symbol, damping, cosine_table, sine_table):
    half_real = planes_second(planes, cosine_table)
    half_imag = -planes_second(planes, sine_table)
    spec_real = planes_first(half_real, cosine_table) + planes_first(half_imag, sine_table)
    spec_imag = planes_first(half_imag, cosine_table) - planes_first(half_real, sine_table)
    mult_real = -damping * spec_real - symbol * spec_imag
    mult_imag = -damping * spec_imag + symbol * spec_real
    back_real = planes_first(mult_real, cosine_table) - planes_first(mult_imag, sine_table)
    back_imag = planes_first(mult_imag, cosine_table) + planes_first(mult_real, sine_table)
    return planes_second(back_real, cosine_table) - planes_second(back_imag, sine_table)


def local(density, mode_waves, mode_amplitudes, mode_phases):
    plane_rows, points, cell_dev = density.shape
    rows_dev = cell_dev // NY
    total_rows = rows_dev * lax.axis_size("space")
    mom_index = lax.axis_index("mom")
    space_index = lax.axis_index("space")
    cosine_table, sine_table = fourier_tables(points)
    indices = jnp.arange(points, dtype=jnp.int32)
    signed = signed_frequency(indices, points)
    speeds = velocity(indices, points)
    first_index = mom_index * plane_rows + jnp.arange(plane_rows, dtype=jnp.int32)
    row_speeds = velocity(first_index, points)
    advection = advect(density, row_speeds, speeds)
    scale = 1.0 / (points * points)
    cell_major = jnp.transpose(density, (2, 0, 1))
    planes = lax.all_to_all(cell_major, "mom", split_axis=0, concat_axis=1, tiled=True)
    group_cells = planes.shape[0]
    local_cells = mom_index * group_cells + jnp.arange(group_cells, dtype=jnp.int32)
    cell_factor = cell_factors(
        mode_waves,
        mode_amplitudes,
        mode_phases,
        space_index * rows_dev + local_cells // NY,
        local_cells % NY,
        total_rows,
        NY,
    )
    freq_factor = freq_factors(mode_waves, signed, signed, points)
    symbol = jnp.dot(cell_factor.T, freq_factor.T, precision=HIGHEST_PRECISION).reshape(
        group_cells, points, points
    )
    damping = damping_table(signed, signed, points)[None, :, :]
    spectral = transform_planes(planes, symbol, damping, cosine_table, sine_table) * scale
    weighted_rows = speeds[None, :, None] * planes
    weighted_columns = speeds[None, None, :] * planes
    padded_rows = jnp.pad(weighted_rows, ((0, 0), (1, 1), (0, 0)))
    padded_columns = jnp.pad(weighted_columns, ((0, 0), (0, 0), (1, 1)))
    friction = FRICTION * (
        padded_rows[:, 2:]
        - padded_rows[:, :-2]
        + (padded_columns[:, :, 2:] - padded_columns[:, :, :-2])
    )
    returned = lax.all_to_all(spectral + friction, "mom", split_axis=1, concat_axis=0, tiled=True)
    momentum_part = jnp.transpose(returned, (1, 2, 0))
    return momentum_part - advection


def solution(mesh):
    return jax.shard_map(
        local,
        mesh=mesh,
        in_specs=(P("mom", None, "space"), P(), P(), P()),
        out_specs=P("mom", None, "space"),
        check_vma=False,
    )
```

profile of v0, /device:TPU:0, one launch (start us, length us, event | category | flops | bytes accessed | tf_op | source)
XLA Modules:
  0.0 349.4 jit_solution(6428627961701099571)
XLA Ops:
  0.0 5.4 %copy.82 = f32[32,256,128]{1,0,2:T(8,128)} copy(f32[32,256,128]{2,1,0:T(8,128)} %param.4) | data formatting | bytes 8388608 | tf_op args[0]
  5.4 0.0 copy-start.4
  5.4 0.0 copy-start.5
  5.4 0.0 copy-start.6
  5.4 6.5 %all-to-all-start = ((f32[128,32,256]{2,1,0:T(8,128)}), f32[128,32,256]{2,1,0:T(8,128)}, u32[]{:S(2)}, u32[]{:S(2)}) async-start(f32[128,32,256]{2,1,0:T(8,128)} %bitcast.118), calls=%async_computation | async-start | bytes 8388608 | tf_op jit(solution)/shard_map/all_to_all | solution.py:155
  11.9 0.0 copy-done.4
  11.9 0.1 broadcast_multiply_fusion.3
  12.0 0.1 copy.90
  12.2 0.1 multiply_negate_fusion
  12.3 0.0 copy-done.5
  12.3 0.0 copy-done.6
  12.3 20.8 %fusion.18 = f32[16,256,256]{2,0,1:T(8,128)} fusion(s32[256,16]{0,1:T(8,128)S(1)} %get-tuple-element.30, s32[256,16]{1,0:T(8,128)S(1)} %copy.90, f32[16]{0:T(128)S(1)} %copy-done.5, s32[16]{0:T(128)S(1)} %get-tuple-element.33, s32[16]{0:T(128)S(1)} %get-tuple-element.32, s32[16]{0:T(128)S(1)} %get-tuple-element.34, s32[16]{0:T(128)S(1)} %get-tuple-element.31, ...), kind=kOutput, calls=%fused_computation.33 | convolution fusion | flops 216014848 | bytes 4227456 | tf_op jit(solution)/shard_map/dot_general | solution.py:168
  33.1 72.9 %all-to-all-done = f32[128,32,256]{2,1,0:T(8,128)} async-done(((f32[128,32,256]{2,1,0:T(8,128)}), f32[128,32,256]{2,1,0:T(8,128)}, u32[]{:S(2)}, u32[]{:S(2)}) %all-to-all-start) | async-done | bytes 4194336 | tf_op jit(solution)/shard_map/all_to_all | solution.py:155
  106.0 2.8 copy.83
  108.8 7.6 %fusion.90 = f32[256,16,256]{2,0,1:T(8,128)S(1)} fusion(f32[16,256,256]{2,1,0:T(8,128)S(1)} %bitcast.116), kind=kOutput, calls=%fused_computation.119 | convolution fusion | flops 3222142976 | bytes 8388608 | tf_op jit(solution)/shard_map/cak,km->cam/dot_general | solution.py:82
  116.4 8.0 %fusion.97 = f32[256,16,256]{2,0,1:T(8,128)S(1)} fusion(f32[16,256,256]{2,1,0:T(8,128)S(1)} %bitcast.117), kind=kOutput, calls=%fused_computation.126 | convolution fusion | flops 3222142976 | bytes 8388608 | tf_op jit(solution)/shard_map/cak,km->cam/dot_general | solution.py:82
  124.4 7.8 %fusion.44 = f32[256,16,256]{2,0,1:T(8,128)S(1)} fusion(f32[256,16,256]{2,0,1:T(8,128)S(1)} %fusion.90), kind=kOutput, calls=%fused_computation.70 | convolution fusion | flops 3223191552 | bytes 8388608 | tf_op jit(solution)/shard_map/ckb,km->cmb/dot_general | solution.py:78
  132.3 7.7 %fusion.42 = f32[256,16,256]{2,0,1:T(8,128)S(1)} fusion(f32[256,16,256]{2,0,1:T(8,128)S(1)} %fusion.90), kind=kOutput, calls=%fused_computation.68 | convolution fusion | flops 3223191552 | bytes 8388608 | tf_op jit(solution)/shard_map/ckb,km->cmb/dot_general | solution.py:78
  140.0 7.8 %fusion.67 = f32[256,16,256]{2,0,1:T(8,128)S(1)} fusion(f32[256,16,256]{2,0,1:T(8,128)S(1)} %fusion.44, f32[256,16,256]{2,0,1:T(8,128)S(1)} %fusion.97), kind=kOutput, calls=%fused_computation.97 | convolution fusion | flops 3223191552 | bytes 12582912 | tf_op jit(solution)/shard_map/ckb,km->cmb/dot_general | solution.py:78
  147.8 14.0 %fusion.40 = (f32[16,256,256]{2,1,0:T(8,128)S(1)}, f32[16,256,256]{2,1,0:T(8,128)S(1)}) fusion(f32[256,16,256]{2,0,1:T(8,128)S(1)} %fusion.67, f32[16,256,256]{2,0,1:T(8,128)} %fusion.18, f32[256,256]{1,0:T(8,128)S(1)} %multiply_negate_fusion, f32[256,16,256]{2,0,1:T(8,128)S(1)} %fusion.42, f32[256,16,256]{2,0,1:T(8,128)S(1)} %fusion.97), kind=kOutput, calls=%fused_computation.64 | convolution fusion | flops 3229483008 | bytes 25427968 | tf_op jit(solution)/shard_map/ckb,km->cmb/dot_general | solution.py:78
  161.8 5.1 %fusion.85 = f32[256,16,256]{2,0,1:T(8,128)S(1)} fusion(f32[16,256,256]{2,1,0:T(8,128)S(1)} %get-tuple-element.5), kind=kOutput, calls=%fused_computation.114 | convolution fusion | flops 3222142976 | bytes 8388608 | tf_op jit(solution)/shard_map/ckb,km->cmb/dot_general | solution.py:78
  166.9 4.8 %fusion.100 = f32[256,16,256]{2,0,1:T(8,128)S(1)} fusion(f32[16,256,256]{2,1,0:T(8,128)S(1)} %get-tuple-element.5), kind=kOutput, calls=%fused_computation.129 | convolution fusion | flops 3222142976 | bytes 8388608 | tf_op jit(solution)/shard_map/ckb,km->cmb/dot_general | solution.py:78
  171.7 5.0 %fusion.93 = f32[256,16,256]{2,0,1:T(8,128)S(1)} fusion(f32[16,256,256]{2,1,0:T(8,128)S(1)} %get-tuple-element.6), kind=kOutput, calls=%fused_computation.122 | convolution fusion | flops 3222142976 | bytes 8388608 | tf_op jit(solution)/shard_map/ckb,km->cmb/dot_general | solution.py:78
  176.7 4.8 %fusion.87 = f32[256,16,256]{2,0,1:T(8,128)S(1)} fusion(f32[16,256,256]{2,1,0:T(8,128)S(1)} %get-tuple-element.6), kind=kOutput, calls=%fused_computation.116 | convolution fusion | flops 3222142976 | bytes 8388608 | tf_op jit(solution)/shard_map/ckb,km->cmb/dot_general | solution.py:78
  181.4 5.2 %broadcast_multiply_fusion.1 = (f32[16,256,256]{2,1,0:T(8,128)}, f32[16,256,256]{2,1,0:T(8,128)}) fusion(f32[256]{0:T(256)S(1)} %convert_multiply_fusion, f32[16,8,32,256]{3,2,1,0:T(8,128)S(1)} %copy.83), kind=kLoop, calls=%fused_computation.100 | loop fusion | flops 2097152 | bytes 12583936 | tf_op jit(solution)/shard_map/mul | solution.py:173
  186.6 4.4 %fusion.36 = f32[16,256,256]{2,1,0:T(8,128)S(1)} fusion(f32[256,16,256]{2,0,1:T(8,128)S(1)} %fusion.93, f32[256,16,256]{2,0,1:T(8,128)S(1)} %fusion.85), kind=kOutput, calls=%fused_computation.58 | convolution fusion | flops 3223191552 | bytes 12582912 | tf_op jit(solution)/shard_map/cak,km->cam/dot_general | solution.py:82
  191.1 13.5 %fusion.23 = f32[16,256,256]{2,1,0:T(8,128)} fusion(f32[16,256,256]{2,1,0:T(8,128)} %get-tuple-element.14, f32[16,256,256]{2,1,0:T(8,128)} %get-tuple-element.13, f32[16,256,256]{2,1,0:T(8,128)S(1)} %fusion.36, f32[256,16,256]{2,0,1:T(8,128)S(1)} %fusion.100, f32[256,16,256]{2,0,1:T(8,128)S(1)} %fusion.87), kind=kOutput, calls=%fused_computation.37 | convolution fusion | flops 3230531584 | bytes 25165824 | tf_op jit(solution)/shard_map/cak,km->cam/dot_general | solution.py:82
  204.6 6.6 %copy.101 = f32[16,256,256]{2,0,1:T(8,128)} copy(f32[16,256,256]{2,1,0:T(8,128)} %fusion.23) | data formatting | bytes 8388608 | tf_op jit(solution)/shard_map/add | solution.py:182
  211.2 4.6 %all-to-all-start.1 = ((f32[16,256,256]{2,0,1:T(8,128)}), f32[16,256,256]{2,0,1:T(8,128)}, u32[]{:S(2)}, u32[]{:S(2)}) async-start(f32[16,256,256]{2,0,1:T(8,128)} %copy.101), calls=%async_computation.1 | async-start | bytes 8388608 | tf_op jit(solution)/shard_map/all_to_all | solution.py:182
  215.7 4.0 %fusion.220 = (f32[32,256,48]{1,0,2:T(8,128)}, f32[32,256,48]{1,0,2:T(8,128)}) fusion(f32[32,256,128]{1,0,2:T(8,128)} %copy.82), kind=kLoop, calls=%fused_computation.261 | loop fusion | bytes 6291456 | tf_op jit(solution)/shard_map/slice | solution.py:22
  219.7 1.5 collective-permute-start
  221.2 1.4 collective-permute-start.1
  222.6 5.9 %copy.109 = f32[32,256,128]{1,2,0:T(8,128)} copy(f32[32,256,128]{2,1,0:T(8,128)} %param.4) | data formatting | bytes 8388608 | tf_op args[0]
  228.5 0.0 copy-start
  228.5 3.6 %fusion.219 = (f32[32,256,8,1]{1,3,2,0:T(1,128)}, f32[32,256,8,1]{1,3,2,0:T(1,128)}) fusion(f32[32,256,8,16]{1,3,2,0:T(8,128)} %bitcast.110), kind=kLoop, calls=%fused_computation.260 | loop fusion | bytes 1048576 | tf_op jit(solution)/shard_map/jit(_roll_static)/slice | solution.py:117
  232.2 3.5 fusion.217
  235.6 3.7 %fusion.214 = (f32[32,256,8,3]{1,3,2,0:T(4,128)}, f32[32,256,8,3]{1,3,2,0:T(4,128)S(1)}) fusion(f32[32,256,8,16]{1,3,2,0:T(8,128)} %bitcast.112), kind=kLoop, calls=%fused_computation.255 | loop fusion | bytes 3145728 | tf_op jit(solution)/shard_map/jit(_roll_static)/slice | solution.py:117
  239.4 0.0 copy-done
  239.4 1.5 fusion.215
  240.9 3.0 fusion.216
  243.8 3.0 fusion.218
  246.8 0.0 copy-start.3
  246.8 7.8 %fusion.33 = (f32[32,256,8,16]{1,3,2,0:T(8,128)}, f32[32,256,8,16]{1,3,2,0:T(8,128)}, f32[32,256,8,16]{1,3,2,0:T(8,128)}) fusion(f32[32,256,8,13]{1,3,2,0:T(8,128)S(1)} %get-tuple-element.17, f32[32,256,8,3]{1,3,2,0:T(4,128)} %get-tuple-element.15, f32[32,256,8,15]{1,3,2,0:T(8,128)} %get-tuple-element.24, f32[32,256,8,1]{1,3,2,0:T(1,128)} %get-tuple-element.26, ...), kind=kLoop, calls=%fused_computation.50 | loop fusion | flops 10485760 | bytes 25165824 | tf_op jit(solution)/shard_map/sub | solution.py:87
  254.7 0.0 copy-done.3
  254.7 5.6 %fusion.65 = (f32[32,256,8,16]{1,3,2,0:T(8,128)}, f32[32,256,8,16]{1,3,2,0:T(8,128)}, f32[32,256,8,16]{1,3,2,0:T(8,128)}) fusion(f32[32,256,8,2]{1,3,2,0:T(2,128)S(1)} %get-tuple-element.21, f32[32,256,8,14]{1,3,2,0:T(8,128)S(1)} %get-tuple-element.19, f32[32,256,8,1]{1,3,2,0:T(1,128)S(1)} %copy-done.3, f32[32,256,8,15]{1,3,2,0:T(8,128)S(1)} %get-tuple-element.23, ...), kind=kLoop, calls=%fused_computation.95 | loop fusion | flops 10485760 | bytes 25165824 | tf_op jit(solution)/shard_map/mul | solution.py:92
  260.3 49.5 %all-to-all-done.1 = f32[16,256,256]{2,0,1:T(8,128)} async-done(((f32[16,256,256]{2,0,1:T(8,128)}), f32[16,256,256]{2,0,1:T(8,128)}, u32[]{:S(2)}, u32[]{:S(2)}) %all-to-all-start.1) | async-done | bytes 4194336 | tf_op jit(solution)/shard_map/all_to_all | solution.py:182
  309.7 0.0 copy-start.1
  309.7 0.0 copy-start.2
  309.7 4.7 %copy.103 = f32[8,16,32,256]{3,2,1,0:T(8,128)S(1)} copy(f32[8,16,32,256]{3,1,2,0:T(8,128)} %bitcast.27) | data formatting | bytes 8388608 | tf_op jit(solution)/shard_map/all_to_all | solution.py:182
  314.5 0.0 collective-permute-done
  314.5 0.0 collective-permute-done.1
  314.5 0.0 copy-done.1
  314.5 0.0 copy-done.2
  314.5 29.1 %fusion.14 = f32[32,256,128]{1,0,2:T(8,128)} fusion(f32[32,256,128]{1,0,2:T(8,128)S(1)} %copy-done.1, f32[32,256,48]{1,0,2:T(8,128)} %collective-permute-done, f32[32,256,48]{1,0,2:T(8,128)} %collective-permute-done.1, f32[8,16,32,256]{3,2,1,0:T(8,128)S(1)} %copy.103, f32[32,256,128]{1,2,0:T(8,128)} %bitcast.120, f32[32,256,128]{1,2,0:T(8,128)} %bitcast.121, ...), kind=kLoop, calls=%fused_computation.29 | loop fusion | flops 45088768 | bytes 40895904 | tf_op jit(solution)/shard_map/sub | solution.py:184
  343.6 5.3 %copy.116 = f32[32,256,128]{2,1,0:T(8,128)} copy(f32[32,256,128]{1,0,2:T(8,128)} %fusion.14) | data formatting | bytes 8388608 | tf_op jit(solution)/shard_map/sub | solution.py:184
  (8 shorter events, 0.1 us)
Async XLA Ops:
  5.4 6.5 %copy-start.4 = (s32[16,2]{0,1:T(2,128)S(1)}, s32[16,2]{0,1:T(2,128)}, u32[]{:S(2)}) copy-start(s32[16,2]{0,1:T(2,128)} %param.5) | copy-start | bytes 388
  5.4 6.8 %copy-start.5 = (f32[16]{0:T(128)S(1)}, f32[16]{0:T(128)}, u32[]{:S(2)}) copy-start(f32[16]{0:T(128)} %param.7) | copy-start | bytes 196
  5.4 6.8 %copy-start.6 = (f32[16]{0:T(128)S(1)}, f32[16]{0:T(128)}, u32[]{:S(2)}) copy-start(f32[16]{0:T(128)} %param.6) | copy-start | bytes 196
  5.4 100.6 %all-to-all-start = ((f32[128,32,256]{2,1,0:T(8,128)}), f32[128,32,256]{2,1,0:T(8,128)}, u32[]{:S(2)}, u32[]{:S(2)}) async-start(f32[128,32,256]{2,1,0:T(8,128)} %bitcast.118), calls=%async_computation | async-start | bytes 8388608 | tf_op jit(solution)/shard_map/all_to_all | solution.py:155
  211.2 98.6 %all-to-all-start.1 = ((f32[16,256,256]{2,0,1:T(8,128)}), f32[16,256,256]{2,0,1:T(8,128)}, u32[]{:S(2)}, u32[]{:S(2)}) async-start(f32[16,256,256]{2,0,1:T(8,128)} %copy.101), calls=%async_computation.1 | async-start | bytes 8388608 | tf_op jit(solution)/shard_map/all_to_all | solution.py:182
  219.7 94.8 %collective-permute-start = (f32[32,256,48]{1,0,2:T(8,128)}, f32[32,256,48]{1,0,2:T(8,128)}, u32[]{:S(2)}, u32[]{:S(2)}) collective-permute-start(f32[32,256,48]{1,0,2:T(8,128)} %get-tuple-element.28), channel_id=1, source_target_pairs={{0,8},{8,16},{16,24},{24,0},{1,9},{9,17},{17,25},{25,1},{2,10},{10... | collective-permute-start | bytes 4718600 | tf_op jit(solution)/shard_map/ppermute | solution.py:23
  221.2 93.3 %collective-permute-start.1 = (f32[32,256,48]{1,0,2:T(8,128)}, f32[32,256,48]{1,0,2:T(8,128)}, u32[]{:S(2)}, u32[]{:S(2)}) collective-permute-start(f32[32,256,48]{1,0,2:T(8,128)} %get-tuple-element.27), channel_id=1, source_target_pairs={{8,0},{16,8},{24,16},{0,24},{9,1},{17,9},{25,17},{1,25},{10,2},{18... | collective-permute-start | bytes 4718600 | tf_op jit(solution)/shard_map/ppermute | solution.py:24
  228.5 10.8 %copy-start = (f32[32,256,128]{1,2,0:T(8,128)S(1)}, f32[32,256,128]{1,2,0:T(8,128)}, u32[]{:S(2)}) copy-start(f32[32,256,128]{1,2,0:T(8,128)} %copy.109) | copy-start | bytes 12582916
  246.8 7.8 %copy-start.3 = (f32[32,256,8,1]{1,3,2,0:T(1,128)S(1)}, f32[32,256,8,1]{1,3,2,0:T(1,128)}, u32[]{:S(2)}) copy-start(f32[32,256,8,1]{1,3,2,0:T(1,128)} %get-tuple-element.25) | copy-start | bytes 786436
  309.7 4.7 %copy-start.1 = (f32[32,256,128]{1,0,2:T(8,128)S(1)}, f32[32,256,128]{1,0,2:T(8,128)}, u32[]{:S(2)}) copy-start(f32[32,256,128]{1,0,2:T(8,128)} %copy.82) | copy-start | bytes 12582916
  309.7 4.8 %copy-start.2 = (f32[32,256,8,16]{1,3,2,0:T(8,128)S(1)}, f32[32,256,8,16]{1,3,2,0:T(8,128)}, u32[]{:S(2)}) copy-start(f32[32,256,8,16]{1,3,2,0:T(8,128)} %get-tuple-element.7) | copy-start | bytes 12582916
where the time goes:
time: 355 us; the launch traced here: 349 us
  waiting for transfers between devices  122 us (34%)
  matrix products  111 us (31%)
  local copies, waits for them, and re-layouts  53 us (15%)
  other arithmetic  48 us (14%)
  starting transfers between devices  14 us (4%)
    all_to_all x1, waiting for transfers between devices, local(): lax.all_to_all(cell_major, 'mom', split_axis=0, concat_axis=1, tiled=True)  72.9 us
    dot_general x8, matrix products, planes_first(): jnp.einsum('ckb,km->cmb', operand, matrix, precision=HIGHEST_PRECISION)  56.9 us
    all_to_all x1, waiting for transfers between devices, local(): lax.all_to_all(spectral + friction, 'mom', split_axis=1, concat_axis=0, t...  49.5 us
    dot_general x4, matrix products, planes_second(): jnp.einsum('cak,km->cam', operand, matrix, precision=HIGHEST_PRECISION)  33.6 us
    sub x1, other arithmetic, local(): return momentum_part - advection  29.1 us
    dot_general x1, matrix products, local(): jnp.dot(cell_factor.T, freq_factor.T, precision=HIGHEST_PRECISION)  20.8 us
    slice x6, local copies, waits for them, and re-layouts, along_row(): jnp.roll(cell_grid, -offset, axis=3).reshape(plane_rows, points, cell_dev)  18.3 us
    unnamed x16, local copies, waits for them, and re-layouts  11.3 us
  transfers between devices with their start and end apart: 4, of which 2 were waited for; matrix products, arithmetic and copies ran while one was open for 19% of the time, Pallas kernels for 0%

commit v1 on v0

v1 whole, which is shorter than its diff:
```python
import functools

import jax
import jax.numpy as jnp
import ml_dtypes
import numpy as np
from jax import lax
from jax.experimental import pallas as pl
from jax.experimental.pallas import tpu as pltpu
from jax.sharding import PartitionSpec as P

NY = 16
PER = 4
ROWS = 2 * PER
DAMPING = 0.5
FRICTION = 0.5
BF16 = jnp.bfloat16
F32 = jnp.float32
MINUS = ((-3, -2.0), (-2, 15.0), (-1, -60.0), (0, 20.0), (1, 30.0), (2, -3.0))
PLUS = ((3, 2.0), (2, -15.0), (1, 60.0), (0, -20.0), (-1, -30.0), (-2, 3.0))


def halves(table):
    high = table.astype(ml_dtypes.bfloat16)
    low = (table - high.astype(np.float64)).astype(ml_dtypes.bfloat16)
    return jnp.asarray(high), jnp.asarray(low)


def mode_order(points, peers):
    per_peer = points // 2 // peers
    return [
        d * per_peer + c * PER + i
        for c in range(per_peer // PER)
        for d in range(peers)
        for i in range(PER)
    ]


def second_tables(points, peers):
    k = np.arange(points)
    forward, back = [], []
    for m in mode_order(points, peers):
        angle = 2.0 * np.pi / points * (k * m % points)
        if m == 0:
            sign = 1.0 - 2.0 * (k % 2)
            forward += [np.ones(points), sign]
            back += [np.ones(points) / points, sign / points]
        else:
            forward += [np.cos(angle), -np.sin(angle)]
            back += [2.0 / points * np.cos(angle), -2.0 / points * np.sin(angle)]
    return np.stack(forward), np.stack(back).T.copy()


def first_tables(points):
    k = np.arange(points)
    turned = k[:, None] * k[None, :] % points
    cosine = np.cos(2.0 * np.pi / points * turned)
    sine = np.sin(2.0 * np.pi / points * turned)
    sine[turned * 2 % points == 0] = 0.0
    return np.concatenate([cosine, sine], 0), np.concatenate([cosine, sine], 1) / points


def row_tables(cells, stencil):
    own = np.zeros((cells, cells))
    left = np.zeros((2, cells, cells))
    right = np.zeros((2, cells, cells))
    half = cells // 2
    for n in range(cells):
        for s, w in stencil:
            src = n + s * NY
            if src < 0:
                for h in range(2):
                    left[h, src + half + h * half, n] += w
            elif src >= cells:
                for h in range(2):
                    right[h, src - cells + h * half, n] += w
            else:
                own[src, n] += w
    return own, np.concatenate(list(left), 1), np.concatenate(list(right), 1)


def column_table(cells, stencil):
    table = np.zeros((cells, cells))
    for n in range(cells):
        for s, w in stencil:
            table[n // NY * NY + (n % NY + s) % NY, n] += w
    return table


def split(value):
    high = value.astype(BF16)
    return high, (value - high.astype(F32)).astype(BF16)


def mm(a, b):
    return jnp.dot(a, b, preferred_element_type=F32)


def left_product(high, low, value):
    vh, vl = split(value)
    return mm(high, vh) + (mm(high, vl) + mm(low, vh))


def exact_product(value, table):
    vh, vl = split(value)
    return mm(vh, table) + mm(vl, table)


def forward_kernel(count, peers, block, x_ref, wh_ref, wl_ref, *outs):
    for a in range(block):
        y = left_product(wh_ref[...], wl_ref[...], x_ref[a])
        for c in range(count):
            for d in range(peers):
                at = (c * peers + d) * ROWS
                outs[c][d, a] = y[at : at + ROWS]


def middle_kernel(
    special, points, cells, flag_ref, x_ref, th_ref, tl_ref, ih_ref, il_ref, a_ref, b_ref, dm_ref, y_ref
):
    row = lax.broadcasted_iota(jnp.int32, (points, 2 * cells), 0)
    speed = (2 * row - (points - 1)).astype(F32) * (FRICTION / points)
    for i in range(PER):
        re = x_ref[pl.ds(2 * i, points, stride=ROWS), :]
        im = x_ref[pl.ds(2 * i + 1, points, stride=ROWS), :]
        x = jnp.concatenate([re, im], axis=1)
        pq = left_product(th_ref[...], tl_ref[...], x)
        pr, pi = pq[:points, :cells], pq[:points, cells:]
        qr, qi = pq[points:, :cells], pq[points:, cells:]
        s = jnp.dot(a_ref[...], b_ref[i], precision=lax.Precision.HIGHEST, preferred_element_type=F32)
        d = dm_ref[i]
        xr, xi = pr + qi, pi - qr
        ur = -d * xr - s * xi
        ui = s * xr - d * xi
        vr, vi = -ui, ur
        if special and i == 0:
            last = jnp.dot(
                a_ref[...], b_ref[PER], precision=lax.Precision.HIGHEST, preferred_element_type=F32
            )
            dl = dm_ref[PER]
            chosen = flag_ref[0] == 0
            ur = jnp.where(chosen, s * qr - d * pr, ur)
            ui = jnp.where(chosen, last * qi - dl * pi, ui)
            vr = jnp.where(chosen, -d * qr - s * pr, vr)
            vi = jnp.where(chosen, -dl * qi - last * pi, vi)
        u = jnp.concatenate([ur, ui], axis=1)
        v = jnp.concatenate([vr, vi], axis=1)
        y = left_product(ih_ref[...], il_ref[...], jnp.concatenate([u, v], axis=0))
        weighted = speed * x
        above = jnp.where(row < points - 1, pltpu.roll(weighted, points - 1, 0), 0.0)
        below = jnp.where(row > 0, pltpu.roll(weighted, 1, 0), 0.0)
        y = y + (above - below)
        y_ref[pl.ds(2 * i, points, stride=ROWS), :] = y[:, :cells]
        y_ref[pl.ds(2 * i + 1, points, stride=ROWS), :] = y[:, cells:]


def local_kernel(points, cells, block, x_ref, l_ref, r_ref, sp_ref, plus_ref, minus_ref, lt_ref, rt_ref, o_ref):
    half = points // 2
    row = lax.broadcasted_iota(jnp.int32, (points, cells), 0)
    speed = (2 * row - (points - 1)).astype(F32) / points
    for a in range(block):
        x = x_ref[a]
        top = exact_product(x[:half], plus_ref[...])
        bottom = exact_product(x[half:], minus_ref[...])
        sides = exact_product(l_ref[a], lt_ref[...]) + exact_product(r_ref[a], rt_ref[...])
        rows = jnp.concatenate([top[:, :cells] + sides[:, :cells], bottom[:, :cells] + sides[:, cells:]], 0)
        columns = jnp.concatenate([top[:, cells:], bottom[:, cells:]], 0)
        weighted = speed * x
        above = jnp.where(row < points - 1, pltpu.roll(weighted, points - 1, 0), 0.0)
        below = jnp.where(row > 0, pltpu.roll(weighted, 1, 0), 0.0)
        first = sp_ref[a]
        o_ref[a] = FRICTION * (above - below) - (first * rows + speed * columns) * (1.0 / 60.0)


def back_kernel(chunks, peers, block, base_ref, wh_ref, wl_ref, *refs):
    ys, o_ref = refs[:chunks], refs[chunks]
    for a in range(block):
        y = jnp.concatenate([ys[c][d, a] for c in range(chunks) for d in range(peers)], axis=0)
        o_ref[a] = base_ref[a] + left_product(wh_ref[...], wl_ref[...], y)


def whole(shape):
    return pl.BlockSpec(shape, lambda *_: (0,) * len(shape))


def params(mib=48):
    return pltpu.CompilerParams(vmem_limit_bytes=mib * 2**20)


def cost(flops, size):
    return pl.CostEstimate(flops=int(flops), bytes_accessed=int(size), transcendentals=0)


def local(density, mode_waves, mode_amplitudes, mode_phases):
    plane_rows, points, cells = density.shape
    rows_dev = cells // NY
    peers = lax.axis_size("mom")
    bands = lax.axis_size("space")
    total_rows = rows_dev * bands
    mom = lax.axis_index("mom")
    space = lax.axis_index("space")
    per_peer = points // 2 // peers
    chunks = per_peer // PER
    block = 8
    steps = plane_rows // block
    half = points // 2
    size = plane_rows * points * cells * 4

    forward, back = second_tables(points, peers)
    bh, bl = halves(back)
    first, inverse = first_tables(points)
    th, tl = halves(first)
    ih, il = halves(inverse)

    def ahead(low, high):
        count = high - low
        part = points // chunks
        wh, wl = halves(forward[low * part : high * part])
        return pl.pallas_call(
            functools.partial(forward_kernel, count, peers, block),
            grid=(steps,),
            out_shape=[jax.ShapeDtypeStruct((peers, plane_rows, ROWS, cells), F32)] * count,
            in_specs=[
                pl.BlockSpec((block, points, cells), lambda g: (g, 0, 0)),
                whole(wh.shape),
                whole(wl.shape),
            ],
            out_specs=[pl.BlockSpec((peers, block, ROWS, cells), lambda g: (0, g, 0, 0))] * count,
            compiler_params=params(),
            cost_estimate=cost(6 * plane_rows * points * cells * part * count, 2 * size),
            name=f"second_transform_{low}",
        )(density, wh, wl)

    sent = list(ahead(0, 1))
    if chunks > 1:
        sent += list(ahead(1, chunks))

    index = jnp.arange(points, dtype=jnp.int32)
    signed = jnp.where(index < half, index, index - points)
    unit = np.float32(np.pi / points)
    a_angle = unit * (mode_waves[None, :, 0] * signed[:, None] % (2 * points)).astype(F32)
    a_sine = jnp.where(index[:, None] == half, 0.0, jnp.sin(a_angle))
    a_table = jnp.concatenate([a_sine, jnp.cos(a_angle)], axis=1)
    cell = jnp.arange(cells, dtype=jnp.int32)
    turn_rows = mode_waves[:, 0:1] * (space * rows_dev + cell // NY)[None, :] % total_rows
    turn_columns = mode_waves[:, 1:2] * (cell % NY)[None, :] % NY
    angles = (
        2.0 * np.pi * (turn_rows.astype(F32) / total_rows + turn_columns.astype(F32) / NY)
        + mode_phases[:, None]
    )
    cell_factor = mode_amplitudes[:, None] * jnp.sin(angles)

    def mode_factors(modes):
        b_angle = unit * (mode_waves[None, :, 1] * modes[:, None] % (2 * points)).astype(F32)
        waves = jnp.concatenate([jnp.cos(b_angle), jnp.sin(b_angle)], axis=1)
        return waves[:, :, None] * jnp.concatenate([cell_factor, cell_factor], axis=0)[None]

    def damping_of(modes):
        squares = (signed * signed)[None, :] + (modes * modes)[:, None]
        values = DAMPING / (half * half) * squares.astype(F32)
        return jnp.broadcast_to(values[:, :, None], (modes.shape[0], points, cells))

    flag = mom.astype(jnp.int32).reshape(1)

    def middle(c, value):
        modes = mom * per_peer + c * PER + jnp.arange(PER, dtype=jnp.int32)
        modes = jnp.concatenate([modes, jnp.full((1,), -half, jnp.int32)])
        vm = pl.BlockSpec(memory_space=pltpu.VMEM)
        return pl.pallas_call(
            functools.partial(middle_kernel, c == 0, points, cells),
            out_shape=jax.ShapeDtypeStruct((points * ROWS, cells), F32),
            in_specs=[pl.BlockSpec(memory_space=pltpu.SMEM)] + [vm] * 8,
            out_specs=vm,
            compiler_params=params(),
            cost_estimate=cost(3 * PER * 16 * points * points * cells, points * ROWS * cells * 12),
            name=f"first_transform_{c}",
        )(
            flag,
            value.reshape(points * ROWS, cells),
            th,
            tl,
            ih,
            il,
            a_table,
            mode_factors(modes),
            damping_of(modes),
        )

    def exchange(value):
        return lax.all_to_all(value, "mom", split_axis=0, concat_axis=0, tiled=True)

    arrived = [exchange(v) for v in sent]

    up = [(i, (i + 1) % bands) for i in range(bands)]
    down = [(j, i) for i, j in up]
    middle_cell = cells // 2

    def packed(part):
        return jnp.concatenate([part[:, :half], part[:, half:]], axis=2)

    before = lax.ppermute(packed(density[:, :, middle_cell:]), "space", up)
    after = lax.ppermute(packed(density[:, :, :middle_cell]), "space", down)
    positive = mom * plane_rows >= half
    own_m, left_m, right_m = row_tables(cells, MINUS)
    own_p, left_p, right_p = row_tables(cells, PLUS)

    def chosen(minus, plus):
        return jnp.where(positive, jnp.asarray(minus, BF16), jnp.asarray(plus, BF16))

    def beside(columns):
        return chosen(np.concatenate([own_m, columns], 1), np.concatenate([own_p, columns], 1))

    speeds = (2 * (mom * plane_rows + jnp.arange(plane_rows, dtype=jnp.int32)) - points + 1).astype(F32) / points
    speeds = jnp.broadcast_to(speeds[:, None, None], (plane_rows, 1, cells))
    plane = lambda g: (g, 0, 0)
    table = whole((cells, 2 * cells))
    base = pl.pallas_call(
        functools.partial(local_kernel, points, cells, block),
        grid=(steps,),
        out_shape=jax.ShapeDtypeStruct(density.shape, F32),
        in_specs=[
            pl.BlockSpec((block, points, cells), plane),
            pl.BlockSpec((block, half, cells), plane),
            pl.BlockSpec((block, half, cells), plane),
            pl.BlockSpec((block, 1, cells), plane),
            table,
            table,
            table,
            table,
        ],
        out_specs=pl.BlockSpec((block, points, cells), plane),
        compiler_params=params(),
        cost_estimate=cost(plane_rows * 16 * half * cells * 2 * cells, 3 * size),
        name="advection_friction",
    )(
        density,
        before,
        after,
        speeds,
        beside(column_table(cells, PLUS)),
        beside(column_table(cells, MINUS)),
        chosen(left_m, left_p),
        chosen(right_m, right_p),
    )

    returned = [
        exchange(middle(c, arrived[c]).reshape(peers, plane_rows, ROWS, cells)) for c in range(chunks)
    ]
    return pl.pallas_call(
        functools.partial(back_kernel, chunks, peers, block),
        grid=(steps,),
        out_shape=jax.ShapeDtypeStruct(density.shape, F32),
        in_specs=[
            pl.BlockSpec((block, points, cells), plane),
            whole(bh.shape),
            whole(bl.shape),
        ]
        + [pl.BlockSpec((peers, block, ROWS, cells), lambda g: (0, g, 0, 0))] * chunks,
        out_specs=pl.BlockSpec((block, points, cells), plane),
        compiler_params=params(),
        cost_estimate=cost(6 * plane_rows * points * points * cells, 3 * size),
        name="second_inverse",
    )(base, bh, bl, *returned)


def solution(mesh):
    return jax.shard_map(
        local,
        mesh=mesh,
        in_specs=(P("mom", None, "space"), P(), P(), P()),
        out_specs=P("mom", None, "space"),
        check_vma=False,
    )
```

time: 355 us -> 312 us (0.88); the launches traced: 349 us -> 310 us
  matrix products: 111 us -> 0 us
  waiting for transfers between devices: 122 us -> 176 us
  other arithmetic: 48 us -> 5.96 us
  Pallas kernels: 0 us -> 38.6 us
  blocking collectives: 0 us -> 29.1 us
  local copies, waits for them, and re-layouts: 53 us -> 27.2 us
  starting transfers between devices: 14 us -> 32.4 us
    dot_general x13 -> x0, matrix products: 111 us -> none  [the longest x8 56.9 us: planes_first(): jnp.einsum('ckb,km->cmb', operand, matrix, precision=HIGHEST_PRECISION)]
    ppermute x2, waiting for transfers between devices: 0.01 us -> 69.4 us  [the longest x1 44.3 us: local(): after = lax.ppermute(packed(density[:, :, :middle_cell]), 'space', down)]
    pallas_call x0 -> x8, Pallas kernels: none -> 38.6 us  [the longest x4 15.4 us: middle(): pl.pallas_call(functools.partial(middle_kernel, c == 0, points, cells), o...]
    sub x2 -> x0, other arithmetic: 36.9 us -> none  [the longest x1 29.1 us: local(): return momentum_part - advection]
    all_to_all x0 -> x1, blocking collectives: none -> 29.1 us  [exchange(): return lax.all_to_all(value, 'mom', split_axis=0, concat_axis=0, tiled=True)]
    all_to_all x2 -> x7, starting transfers between devices: 11 us -> 29.5 us  [exchange(): return lax.all_to_all(value, 'mom', split_axis=0, concat_axis=0, tiled=True)]
    slice x7 -> x1, local copies, waits for them, and re-layouts: 22.3 us -> 5.03 us  [packed(): return jnp.concatenate([part[:, :half], part[:, half:]], axis=2)]
    all_to_all x2 -> x7, waiting for transfers between devices: 122 us -> 107 us  [exchange(): return lax.all_to_all(value, 'mom', split_axis=0, concat_axis=0, tiled=True)]
  transfers between devices with their start and end apart: 4 -> 9, of which waited for: 2 -> 8; matrix products, arithmetic and copies ran while one was open for 19% -> 4% of each run, Pallas kernels for 0% -> 9%
where the time goes in v1:
time: 312 us; the launch traced here: 310 us
  waiting for transfers between devices  176 us (56%)
  Pallas kernels  38.6 us (12%)
  starting transfers between devices  32.4 us (10%)
  blocking collectives  29.1 us (9%)
  local copies, waits for them, and re-layouts  27.2 us (9%)
  other arithmetic  5.96 us (2%)
    all_to_all x7, waiting for transfers between devices, exchange(): return lax.all_to_all(value, 'mom', split_axis=0, concat_axis=0, tiled=True)  107 us
    ppermute x1, waiting for transfers between devices, local(): after = lax.ppermute(packed(density[:, :, :middle_cell]), 'space', down)  44.3 us
    all_to_all x7, starting transfers between devices, exchange(): return lax.all_to_all(value, 'mom', split_axis=0, concat_axis=0, tiled=True)  29.5 us
    all_to_all x1, blocking collectives, exchange(): return lax.all_to_all(value, 'mom', split_axis=0, concat_axis=0, tiled=True)  29.1 us
    ppermute x1, waiting for transfers between devices, local(): before = lax.ppermute(packed(density[:, :, middle_cell:]), 'space', up)  25.1 us
    unnamed x76, local copies, waits for them, and re-layouts  21.1 us
    pallas_call x4, Pallas kernels, middle(): pl.pallas_call(functools.partial(middle_kernel, c == 0, points, cells), o...  15.4 us
    pallas_call x1, Pallas kernels, local(): pl.pallas_call(functools.partial(local_kernel, points, cells, block), gri...  8.63 us
  transfers between devices with their start and end apart: 9, of which 8 were waited for; matrix products, arithmetic and copies ran while one was open for 4% of the time, Pallas kernels for 9%

profile of v1, /device:TPU:0, one launch (start us, length us, event | category | flops | bytes accessed | tf_op | source)
XLA Modules:
  0.0 310.1 jit_solution(14524446446292872448)
XLA Ops:
  0.0 2.2 copy-done
  2.2 0.8 copy-done.9
  2.9 0.8 copy-done.10
  3.7 2.5 second_transform_0.1
  6.2 6.5 %all-to-all-start = ((f32[8,32,8,128]{3,2,1,0:T(8,128)}), f32[8,32,8,128]{3,2,1,0:T(8,128)S(1)}, u32[]{:S(2)}, u32[]{:S(2)}) async-start(f32[8,32,8,128]{3,2,1,0:T(8,128)} %second_transform_0.1), calls=%async_computation | async-start | bytes 2097152 | tf_op jit(solution)/shard_map/all_to_all | solution.py:290
  12.7 5.0 %second_transform_1.1 = (f32[8,32,8,128]{3,2,1,0:T(8,128)S(1)}, f32[8,32,8,128]{3,2,1,0:T(8,128)S(1)}, f32[8,32,8,128]{3,2,1,0:T(8,128)S(1)}) custom-call(f32[32,256,128]{2,1,0:T(8,128)} %x_ref.5, bf16[192,256]{1,0:T(8,128)(2,1)S(1)} %copy-done.27, bf16[192,256]{1,0:T(8,128)(2,1)S(1)} %copy-done.28), custom_call_target="tpu_custom_call" | custom-call | flops 1207959552 | bytes 8388608 | tf_op jit(solution)/shard_map/second_transform_1/pallas_call | solution.py:219
  17.7 1.0 copy-done.1
  18.7 1.0 copy-done.2
  19.7 19.6 %all-to-all-done = f32[8,32,8,128]{3,2,1,0:T(8,128)S(1)} async-done(((f32[8,32,8,128]{3,2,1,0:T(8,128)}), f32[8,32,8,128]{3,2,1,0:T(8,128)S(1)}, u32[]{:S(2)}, u32[]{:S(2)}) %all-to-all-start) | async-done | bytes 1048608 | tf_op jit(solution)/shard_map/all_to_all | solution.py:290
  39.3 29.1 %all_to_all.40 = f32[8,32,8,128]{3,2,1,0:T(8,128)S(1)} all-to-all(f32[8,32,8,128]{3,2,1,0:T(8,128)S(1)} %get-tuple-element.8), channel_id=1, replica_groups=mesh['space'=4,'mom'=8] {'mom'}, dimensions={0} | all-to-all | bytes 2097152 | tf_op jit(solution)/shard_map/all_to_all | solution.py:290
  68.4 3.7 %all-to-all-start.4 = ((f32[8,32,8,128]{3,2,1,0:T(8,128)}), f32[8,32,8,128]{3,2,1,0:T(8,128)S(1)}, u32[]{:S(2)}, u32[]{:S(2)}) async-start(f32[8,32,8,128]{3,2,1,0:T(8,128)} %copy-done.2), calls=%async_computation.4 | async-start | bytes 2097152 | tf_op jit(solution)/shard_map/all_to_all | solution.py:290
  72.2 0.2 sine_select_fusion
  72.3 0.1 copy.23.a_ref
  72.5 0.1 fusion.39
  72.6 26.0 %all-to-all-done.4 = f32[8,32,8,128]{3,2,1,0:T(8,128)S(1)} async-done(((f32[8,32,8,128]{3,2,1,0:T(8,128)}), f32[8,32,8,128]{3,2,1,0:T(8,128)S(1)}, u32[]{:S(2)}, u32[]{:S(2)}) %all-to-all-start.4) | async-done | bytes 1048608 | tf_op jit(solution)/shard_map/all_to_all | solution.py:290
  98.6 4.2 %all-to-all-start.6 = ((f32[8,32,8,128]{3,2,1,0:T(8,128)}), f32[8,32,8,128]{3,2,1,0:T(8,128)}, u32[]{:S(2)}, u32[]{:S(2)}) async-start(f32[8,32,8,128]{3,2,1,0:T(8,128)} %copy-done.1), calls=%async_computation.6 | async-start | bytes 2097152 | tf_op jit(solution)/shard_map/all_to_all | solution.py:290
  102.9 0.1 fusion.37
  103.0 0.2 fusion.28
  103.4 0.1 fusion.9
  103.6 0.1 convert_multiply_fusion
  103.7 0.1 broadcast_multiply_fusion
  103.8 0.2 broadcast_in_dim.25.dm_ref
  104.1 0.9 copy-done.11
  105.0 0.9 copy-done.15
  106.0 0.9 copy-done.19
  106.9 0.9 copy-done.23
  107.9 3.6 %first_transform_0.1 = f32[2048,128]{1,0:T(8,128)S(1)} custom-call(s32[1]{0:T(128)} %bitcast.flag_ref, f32[2048,128]{1,0:T(8,128)S(1)} %bitcast.14, bf16[512,256]{1,0:T(8,128)(2,1)S(1)} %copy-done.11, bf16[512,256]{1,0:T(8,128)(2,1)S(1)} %copy-done.15, bf16[256,512]{1,0:T(8,128)(2,1)S(1)} %copy-done.19, bf16[256,512]{1,0:T(8,128)(2,1)S(1)} %copy-done.23, ...), custom_call_target="tpu_custom_call" | custom-call | flops 1610612736 | bytes 3145728 | tf_op jit(solution)/shard_map/first_transform_0/pallas_call | solution.py:269
  111.5 1.0 copy-done.5
  112.4 17.1 %all-to-all-done.6 = f32[8,32,8,128]{3,2,1,0:T(8,128)} async-done(((f32[8,32,8,128]{3,2,1,0:T(8,128)}), f32[8,32,8,128]{3,2,1,0:T(8,128)}, u32[]{:S(2)}, u32[]{:S(2)}) %all-to-all-start.6) | async-done | bytes 1048608 | tf_op jit(solution)/shard_map/all_to_all | solution.py:290
  129.5 3.6 %all-to-all-start.1 = ((f32[8,32,8,128]{3,2,1,0:T(8,128)}), f32[8,32,8,128]{3,2,1,0:T(8,128)S(1)}, u32[]{:S(2)}, u32[]{:S(2)}) async-start(f32[8,32,8,128]{3,2,1,0:T(8,128)} %bitcast.18), calls=%async_computation.1 | async-start | bytes 2097152 | tf_op jit(solution)/shard_map/all_to_all | solution.py:290
  133.0 0.2 broadcast_in_dim.26.dm_ref
  133.3 0.9 copy-done.12
  134.2 0.9 copy-done.16
  135.2 0.9 copy-done.20
  136.1 0.9 copy-done.24
  137.1 3.5 %first_transform_1.1 = f32[2048,128]{1,0:T(8,128)S(1)} custom-call(s32[1]{0:T(128)} %bitcast.flag_ref, f32[2048,128]{1,0:T(8,128)S(1)} %bitcast.15, bf16[512,256]{1,0:T(8,128)(2,1)S(1)} %copy-done.12, bf16[512,256]{1,0:T(8,128)(2,1)S(1)} %copy-done.16, bf16[256,512]{1,0:T(8,128)(2,1)S(1)} %copy-done.20, bf16[256,512]{1,0:T(8,128)(2,1)S(1)} %copy-done.24, ...), custom_call_target="tpu_custom_call" | custom-call | flops 1610612736 | bytes 3145728 | tf_op jit(solution)/shard_map/first_transform_1/pallas_call | solution.py:269
  140.6 1.0 copy-done.6
  141.6 17.9 %all-to-all-done.1.refs_0_ = f32[8,32,8,128]{3,2,1,0:T(8,128)S(1)} async-done(((f32[8,32,8,128]{3,2,1,0:T(8,128)}), f32[8,32,8,128]{3,2,1,0:T(8,128)S(1)}, u32[]{:S(2)}, u32[]{:S(2)}) %all-to-all-start.1) | async-done | bytes 1048608 | tf_op jit(solution)/shard_map/all_to_all | solution.py:290
  159.6 3.6 %all-to-all-start.3 = ((f32[8,32,8,128]{3,2,1,0:T(8,128)}), f32[8,32,8,128]{3,2,1,0:T(8,128)S(1)}, u32[]{:S(2)}, u32[]{:S(2)}) async-start(f32[8,32,8,128]{3,2,1,0:T(8,128)} %bitcast.19), calls=%async_computation.3 | async-start | bytes 2097152 | tf_op jit(solution)/shard_map/all_to_all | solution.py:290
  163.1 0.2 broadcast_in_dim.27.dm_ref
  163.4 0.9 copy-done.13
  164.3 0.9 copy-done.17
  165.3 0.9 copy-done.21
  166.2 0.9 copy-done.25
  167.2 3.5 %first_transform_2.1 = f32[2048,128]{1,0:T(8,128)S(1)} custom-call(s32[1]{0:T(128)} %bitcast.flag_ref, f32[2048,128]{1,0:T(8,128)S(1)} %bitcast.13, bf16[512,256]{1,0:T(8,128)(2,1)S(1)} %copy-done.13, bf16[512,256]{1,0:T(8,128)(2,1)S(1)} %copy-done.17, bf16[256,512]{1,0:T(8,128)(2,1)S(1)} %copy-done.21, bf16[256,512]{1,0:T(8,128)(2,1)S(1)} %copy-done.25, ...), custom_call_target="tpu_custom_call" | custom-call | flops 1610612736 | bytes 3145728 | tf_op jit(solution)/shard_map/first_transform_2/pallas_call | solution.py:269
  170.7 1.0 copy-done.4
  171.7 18.0 %all-to-all-done.3.refs_1_ = f32[8,32,8,128]{3,2,1,0:T(8,128)S(1)} async-done(((f32[8,32,8,128]{3,2,1,0:T(8,128)}), f32[8,32,8,128]{3,2,1,0:T(8,128)S(1)}, u32[]{:S(2)}, u32[]{:S(2)}) %all-to-all-start.3) | async-done | bytes 1048608 | tf_op jit(solution)/shard_map/all_to_all | solution.py:290
  189.6 3.7 %all-to-all-start.5 = ((f32[8,32,8,128]{3,2,1,0:T(8,128)}), f32[8,32,8,128]{3,2,1,0:T(8,128)S(1)}, u32[]{:S(2)}, u32[]{:S(2)}) async-start(f32[8,32,8,128]{3,2,1,0:T(8,128)} %bitcast.17), calls=%async_computation.5 | async-start | bytes 2097152 | tf_op jit(solution)/shard_map/all_to_all | solution.py:290
  193.4 5.0 %fusion.41 = (f32[32,128,64]{2,1,0:T(8,128)S(1)}, f32[32,128,64]{2,1,0:T(8,128)S(1)}, f32[32,128,64]{2,1,0:T(8,128)S(1)}, f32[32,128,64]{2,1,0:T(8,128)S(1)}) fusion(f32[32,256,128]{2,1,0:T(8,128)} %x_ref.5), kind=kLoop, calls=%fused_computation.115 | loop fusion | bytes 8388608 | tf_op jit(solution)/shard_map/slice | solution.py:299
  198.4 1.9 pad_maximum_fusion
  200.4 1.5 collective-permute-start
  201.9 2.0 pad_maximum_fusion.1
  203.8 1.4 collective-permute-start.1
  205.2 0.2 broadcast_in_dim.28.dm_ref
  205.5 4.8 %first_transform_3.1 = f32[2048,128]{1,0:T(8,128)S(1)} custom-call(s32[1]{0:T(128)} %bitcast.flag_ref, f32[2048,128]{1,0:T(8,128)} %bitcast.9.x_ref, bf16[512,256]{1,0:T(8,128)(2,1)S(1)} %copy-done.14, bf16[512,256]{1,0:T(8,128)(2,1)S(1)} %copy-done.18, bf16[256,512]{1,0:T(8,128)(2,1)S(1)} %copy-done.22, bf16[256,512]{1,0:T(8,128)(2,1)S(1)} %copy-done.26, ...), custom_call_target="tpu_custom_call" | custom-call | flops 1610612736 | bytes 3145728 | tf_op jit(solution)/shard_map/first_transform_3/pallas_call | solution.py:269
  210.3 1.0 copy-done.3
  211.3 8.4 %all-to-all-done.5.refs_2_ = f32[8,32,8,128]{3,2,1,0:T(8,128)S(1)} async-done(((f32[8,32,8,128]{3,2,1,0:T(8,128)}), f32[8,32,8,128]{3,2,1,0:T(8,128)S(1)}, u32[]{:S(2)}, u32[]{:S(2)}) %all-to-all-start.5) | async-done | bytes 1048608 | tf_op jit(solution)/shard_map/all_to_all | solution.py:290
  219.7 4.2 %all-to-all-start.7 = ((f32[8,32,8,128]{3,2,1,0:T(8,128)}), f32[8,32,8,128]{3,2,1,0:T(8,128)}, u32[]{:S(2)}, u32[]{:S(2)}) async-start(f32[8,32,8,128]{3,2,1,0:T(8,128)} %bitcast.16), calls=%async_computation.7 | async-start | bytes 2097152 | tf_op jit(solution)/shard_map/all_to_all | solution.py:290
  224.0 0.9 broadcast_select_fusion.2
  224.9 25.1 %collective-permute-done.l_ref = f32[32,128,128]{2,1,0:T(8,128)} collective-permute-done((f32[32,128,128]{2,1,0:T(8,128)}, f32[32,128,128]{2,1,0:T(8,128)}, u32[]{:S(2)}, u32[]{:S(2)}) %collective-permute-start) | collective-permute-done | bytes 2097184 | tf_op jit(solution)/shard_map/ppermute | solution.py:301
  250.0 44.3 %collective-permute-done.1.r_ref = f32[32,128,128]{2,1,0:T(8,128)} collective-permute-done((f32[32,128,128]{2,1,0:T(8,128)}, f32[32,128,128]{2,1,0:T(8,128)}, u32[]{:S(2)}, u32[]{:S(2)}) %collective-permute-start.1) | collective-permute-done | bytes 2097184 | tf_op jit(solution)/shard_map/ppermute | solution.py:302
  294.3 0.1 broadcast_in_dim.22.sp_ref
  294.4 8.6 %advection_friction.1.base_ref = f32[32,256,128]{2,1,0:T(8,128)} custom-call(f32[32,256,128]{2,1,0:T(8,128)} %x_ref.5, f32[32,128,128]{2,1,0:T(8,128)} %collective-permute-done.l_ref, f32[32,128,128]{2,1,0:T(8,128)} %collective-permute-done.1.r_ref, f32[32,1,128]{2,1,0:T(1,128)S(1)} %broadcast_in_dim.22.sp_ref, ...), custom_call_target="tpu_custom_call" | custom-call | flops 2147483648 | bytes 12582912 | tf_op jit(solution)/shard_map/advection_friction/pallas_call | solution.py:317
  303.1 7.0 %second_inverse.1 = f32[32,256,128]{2,1,0:T(8,128)} custom-call(f32[32,256,128]{2,1,0:T(8,128)} %advection_friction.1.base_ref, bf16[256,256]{1,0:T(8,128)(2,1)S(1)} %copy-done.7, bf16[256,256]{1,0:T(8,128)(2,1)S(1)} %copy-done.8, f32[8,32,8,128]{3,2,1,0:T(8,128)S(1)} %all-to-all-done.1.refs_0_, f32[8,32,8,128]{3,2,1,0:T(8,128)S(1)} %all-to-all-done.3.refs_1_, ...), custom_call_target="tpu_custom_call" | custom-call | flops 1610612736 | bytes 12582912 | tf_op jit(solution)/shard_map/second_inverse/pallas_call | solution.py:349
  (73 shorter events, 0.5 us)
Async XLA Ops:
  0.0 2.2 copy-start
  2.2 0.8 copy-start.9
  2.9 0.8 copy-start.10
  6.2 6.5 %copy-start.27 = (bf16[192,256]{1,0:T(8,128)(2,1)S(1)}, bf16[192,256]{1,0:T(8,128)(2,1)}, u32[]{:S(2)}) copy-start(bf16[192,256]{1,0:T(8,128)(2,1)} %constant.186.clone.wh_ref) | copy-start | bytes 294916
  6.2 6.5 %copy-start.28 = (bf16[192,256]{1,0:T(8,128)(2,1)S(1)}, bf16[192,256]{1,0:T(8,128)(2,1)}, u32[]{:S(2)}) copy-start(bf16[192,256]{1,0:T(8,128)(2,1)} %constant.187.clone.wl_ref) | copy-start | bytes 294916
  6.2 33.1 %all-to-all-start = ((f32[8,32,8,128]{3,2,1,0:T(8,128)}), f32[8,32,8,128]{3,2,1,0:T(8,128)S(1)}, u32[]{:S(2)}, u32[]{:S(2)}) async-start(f32[8,32,8,128]{3,2,1,0:T(8,128)} %second_transform_0.1), calls=%async_computation | async-start | bytes 2097152 | tf_op jit(solution)/shard_map/all_to_all | solution.py:290
  17.7 1.0 copy-start.1
  18.7 1.0 copy-start.2
  39.3 32.9 %copy-start.35 = (s32[16,2]{0,1:T(2,128)S(1)}, s32[16,2]{0,1:T(2,128)}, u32[]{:S(2)}) copy-start(s32[16,2]{0,1:T(2,128)} %param.23) | copy-start | bytes 388
  68.4 35.0 %copy-start.36 = (f32[16]{0:T(128)S(1)}, f32[16]{0:T(128)}, u32[]{:S(2)}) copy-start(f32[16]{0:T(128)} %param.25) | copy-start | bytes 196
  68.4 35.0 %copy-start.37 = (f32[16]{0:T(128)S(1)}, f32[16]{0:T(128)}, u32[]{:S(2)}) copy-start(f32[16]{0:T(128)} %param.24) | copy-start | bytes 196
  68.4 30.2 %all-to-all-start.4 = ((f32[8,32,8,128]{3,2,1,0:T(8,128)}), f32[8,32,8,128]{3,2,1,0:T(8,128)S(1)}, u32[]{:S(2)}, u32[]{:S(2)}) async-start(f32[8,32,8,128]{3,2,1,0:T(8,128)} %copy-done.2), calls=%async_computation.4 | async-start | bytes 2097152 | tf_op jit(solution)/shard_map/all_to_all | solution.py:290
  98.6 30.8 %all-to-all-start.6 = ((f32[8,32,8,128]{3,2,1,0:T(8,128)}), f32[8,32,8,128]{3,2,1,0:T(8,128)}, u32[]{:S(2)}, u32[]{:S(2)}) async-start(f32[8,32,8,128]{3,2,1,0:T(8,128)} %copy-done.1), calls=%async_computation.6 | async-start | bytes 2097152 | tf_op jit(solution)/shard_map/all_to_all | solution.py:290
  104.0 1.0 copy-start.11
  105.0 0.9 copy-start.15
  106.0 0.9 copy-start.19
  106.9 0.9 copy-start.23
  111.4 1.0 copy-start.5
  129.5 30.1 %all-to-all-start.1 = ((f32[8,32,8,128]{3,2,1,0:T(8,128)}), f32[8,32,8,128]{3,2,1,0:T(8,128)S(1)}, u32[]{:S(2)}, u32[]{:S(2)}) async-start(f32[8,32,8,128]{3,2,1,0:T(8,128)} %bitcast.18), calls=%async_computation.1 | async-start | bytes 2097152 | tf_op jit(solution)/shard_map/all_to_all | solution.py:290
  133.3 1.0 copy-start.12
  134.2 0.9 copy-start.16
  135.2 0.9 copy-start.20
  136.1 0.9 copy-start.24
  140.6 1.0 copy-start.6
  159.6 30.1 %all-to-all-start.3 = ((f32[8,32,8,128]{3,2,1,0:T(8,128)}), f32[8,32,8,128]{3,2,1,0:T(8,128)S(1)}, u32[]{:S(2)}, u32[]{:S(2)}) async-start(f32[8,32,8,128]{3,2,1,0:T(8,128)} %bitcast.19), calls=%async_computation.3 | async-start | bytes 2097152 | tf_op jit(solution)/shard_map/all_to_all | solution.py:290
  163.3 1.0 copy-start.13
  164.3 0.9 copy-start.17
  165.3 0.9 copy-start.21
  166.2 0.9 copy-start.25
  170.7 1.0 copy-start.4
  189.6 30.1 %all-to-all-start.5 = ((f32[8,32,8,128]{3,2,1,0:T(8,128)}), f32[8,32,8,128]{3,2,1,0:T(8,128)S(1)}, u32[]{:S(2)}, u32[]{:S(2)}) async-start(f32[8,32,8,128]{3,2,1,0:T(8,128)} %bitcast.17), calls=%async_computation.5 | async-start | bytes 2097152 | tf_op jit(solution)/shard_map/all_to_all | solution.py:290
  200.4 49.7 %collective-permute-start = (f32[32,128,128]{2,1,0:T(8,128)}, f32[32,128,128]{2,1,0:T(8,128)}, u32[]{:S(2)}, u32[]{:S(2)}) collective-permute-start(f32[32,128,128]{2,1,0:T(8,128)} %pad_maximum_fusion), channel_id=1, source_target_pairs={{0,8},{8,16},{16,24},{24,0},{1,9},{9,17},{17,25},{25,1},{2,10},{10... | collective-permute-start | bytes 6291464 | tf_op jit(solution)/shard_map/ppermute | solution.py:301
  201.9 3.6 %copy-start.14 = (bf16[512,256]{1,0:T(8,128)(2,1)S(1)}, bf16[512,256]{1,0:T(8,128)(2,1)}, u32[]{:S(2)}) copy-start(bf16[512,256]{1,0:T(8,128)(2,1)} %constant.180.clone.th_ref) | copy-start | bytes 786436
  201.9 3.6 %copy-start.18 = (bf16[512,256]{1,0:T(8,128)(2,1)S(1)}, bf16[512,256]{1,0:T(8,128)(2,1)}, u32[]{:S(2)}) copy-start(bf16[512,256]{1,0:T(8,128)(2,1)} %constant.181.clone.tl_ref) | copy-start | bytes 786436
  201.9 3.6 %copy-start.22 = (bf16[256,512]{1,0:T(8,128)(2,1)S(1)}, bf16[256,512]{1,0:T(8,128)(2,1)}, u32[]{:S(2)}) copy-start(bf16[256,512]{1,0:T(8,128)(2,1)} %constant.182.clone.ih_ref) | copy-start | bytes 786436
  201.9 3.6 %copy-start.26 = (bf16[256,512]{1,0:T(8,128)(2,1)S(1)}, bf16[256,512]{1,0:T(8,128)(2,1)}, u32[]{:S(2)}) copy-start(bf16[256,512]{1,0:T(8,128)(2,1)} %constant.183.clone.il_ref) | copy-start | bytes 786436
  203.8 90.5 %collective-permute-start.1 = (f32[32,128,128]{2,1,0:T(8,128)}, f32[32,128,128]{2,1,0:T(8,128)}, u32[]{:S(2)}, u32[]{:S(2)}) collective-permute-start(f32[32,128,128]{2,1,0:T(8,128)} %pad_maximum_fusion.1), channel_id=1, source_target_pairs={{8,0},{16,8},{24,16},{0,24},{9,1},{17,9},{25,17},{1,25},{10,2},{18... | collective-permute-start | bytes 6291464 | tf_op jit(solution)/shard_map/ppermute | solution.py:302
  210.3 1.0 copy-start.3
  211.2 12.7 %copy-start.33 = (bf16[128,256]{1,0:T(8,128)(2,1)S(1)}, bf16[128,256]{1,0:T(8,128)(2,1)}, u32[]{:S(2)}) copy-start(bf16[128,256]{1,0:T(8,128)(2,1)} %constant.190.clone) | copy-start | bytes 196612
  211.2 12.8 %copy-start.34 = (bf16[128,256]{1,0:T(8,128)(2,1)S(1)}, bf16[128,256]{1,0:T(8,128)(2,1)}, u32[]{:S(2)}) copy-start(bf16[128,256]{1,0:T(8,128)(2,1)} %constant.191.clone) | copy-start | bytes 196612
  211.2 13.6 %copy-start.29 = (bf16[128,256]{1,0:T(8,128)(2,1)S(1)}, bf16[128,256]{1,0:T(8,128)(2,1)}, u32[]{:S(2)}) copy-start(bf16[128,256]{1,0:T(8,128)(2,1)} %constant.194.clone) | copy-start | bytes 196612
  211.2 13.6 %copy-start.30 = (bf16[128,256]{1,0:T(8,128)(2,1)S(1)}, bf16[128,256]{1,0:T(8,128)(2,1)}, u32[]{:S(2)}) copy-start(bf16[128,256]{1,0:T(8,128)(2,1)} %constant.195.clone) | copy-start | bytes 196612
  211.3 13.6 %copy-start.31 = (bf16[128,256]{1,0:T(8,128)(2,1)S(1)}, bf16[128,256]{1,0:T(8,128)(2,1)}, u32[]{:S(2)}) copy-start(bf16[128,256]{1,0:T(8,128)(2,1)} %constant.192.clone) | copy-start | bytes 196612
  211.3 13.6 %copy-start.32 = (bf16[128,256]{1,0:T(8,128)(2,1)S(1)}, bf16[128,256]{1,0:T(8,128)(2,1)}, u32[]{:S(2)}) copy-start(bf16[128,256]{1,0:T(8,128)(2,1)} %constant.193.clone) | copy-start | bytes 196612
  219.7 83.4 %all-to-all-start.7 = ((f32[8,32,8,128]{3,2,1,0:T(8,128)}), f32[8,32,8,128]{3,2,1,0:T(8,128)}, u32[]{:S(2)}, u32[]{:S(2)}) async-start(f32[8,32,8,128]{3,2,1,0:T(8,128)} %bitcast.16), calls=%async_computation.7 | async-start | bytes 2097152 | tf_op jit(solution)/shard_map/all_to_all | solution.py:290
  294.4 8.7 %copy-start.7 = (bf16[256,256]{1,0:T(8,128)(2,1)S(1)}, bf16[256,256]{1,0:T(8,128)(2,1)}, u32[]{:S(2)}) copy-start(bf16[256,256]{1,0:T(8,128)(2,1)} %constant.178.clone.wh_ref) | copy-start | bytes 393220
  294.4 8.7 %copy-start.8 = (bf16[256,256]{1,0:T(8,128)(2,1)S(1)}, bf16[256,256]{1,0:T(8,128)(2,1)}, u32[]{:S(2)}) copy-start(bf16[256,256]{1,0:T(8,128)(2,1)} %constant.179.clone.wl_ref) | copy-start | bytes 393220

commit v2 on v1

v2 whole, which is shorter than its diff:
```python
import functools

import jax
import jax.numpy as jnp
import ml_dtypes
import numpy as np
from jax import lax
from jax.experimental import pallas as pl
from jax.experimental.pallas import tpu as pltpu
from jax.sharding import PartitionSpec as P

NY = 16
PER = 4
ROWS = 2 * PER
DAMPING = 0.5
FRICTION = 0.5
BF16 = jnp.bfloat16
F32 = jnp.float32
MINUS = ((-3, -2.0), (-2, 15.0), (-1, -60.0), (0, 20.0), (1, 30.0), (2, -3.0))
PLUS = ((3, 2.0), (2, -15.0), (1, 60.0), (0, -20.0), (-1, -30.0), (-2, 3.0))


def halves(table):
    high = table.astype(ml_dtypes.bfloat16)
    low = (table - high.astype(np.float64)).astype(ml_dtypes.bfloat16)
    return jnp.asarray(high), jnp.asarray(low)


def mode_order(points, peers):
    per_peer = points // 2 // peers
    return [
        d * per_peer + c * PER + i
        for c in range(per_peer // PER)
        for d in range(peers)
        for i in range(PER)
    ]


def second_tables(points, peers):
    k = np.arange(points)
    forward, back = [], []
    for m in mode_order(points, peers):
        angle = 2.0 * np.pi / points * (k * m % points)
        if m == 0:
            sign = 1.0 - 2.0 * (k % 2)
            forward += [np.ones(points), sign]
            back += [np.ones(points) / points, sign / points]
        else:
            forward += [np.cos(angle), -np.sin(angle)]
            back += [2.0 / points * np.cos(angle), -2.0 / points * np.sin(angle)]
    return np.stack(forward), np.stack(back).T.copy()


def first_tables(points):
    k = np.arange(points)
    turned = k[:, None] * k[None, :] % points
    cosine = np.cos(2.0 * np.pi / points * turned)
    sine = np.sin(2.0 * np.pi / points * turned)
    sine[turned * 2 % points == 0] = 0.0
    return np.concatenate([cosine, sine], 0), np.concatenate([cosine, sine], 1) / points


def row_tables(cells, stencil):
    own = np.zeros((cells, cells))
    left = np.zeros((2, cells, cells))
    right = np.zeros((2, cells, cells))
    half = cells // 2
    for n in range(cells):
        for s, w in stencil:
            src = n + s * NY
            if src < 0:
                for h in range(2):
                    left[h, src + half + h * half, n] += w
            elif src >= cells:
                for h in range(2):
                    right[h, src - cells + h * half, n] += w
            else:
                own[src, n] += w
    return own, np.concatenate(list(left), 1), np.concatenate(list(right), 1)


def column_table(cells, stencil):
    table = np.zeros((cells, cells))
    for n in range(cells):
        for s, w in stencil:
            table[n // NY * NY + (n % NY + s) % NY, n] += w
    return table


def split(value):
    high = value.astype(BF16)
    return high, (value - high.astype(F32)).astype(BF16)


def mm(a, b):
    return jnp.dot(a, b, preferred_element_type=F32)


def left_product(high, low, value):
    vh, vl = split(value)
    return mm(high, vh) + (mm(high, vl) + mm(low, vh))


def exact_product(value, table):
    vh, vl = split(value)
    return mm(vh, table) + mm(vl, table)


def difference(weighted, row, points):
    above = jnp.where(row < points - 1, pltpu.roll(weighted, points - 1, 0), 0.0)
    below = jnp.where(row > 0, pltpu.roll(weighted, 1, 0), 0.0)
    return above - below


def exchange_kernel(
    peers,
    bands,
    chunks,
    plane_rows,
    points,
    cells,
    x_ref,
    wh_ref,
    wl_ref,
    th_ref,
    tl_ref,
    ih_ref,
    il_ref,
    a_ref,
    b_ref,
    plus_ref,
    minus_ref,
    lt_ref,
    rt_ref,
    bh_ref,
    bl_ref,
    out_ref,
    last_ref,
    xs,
    xr,
    ys,
    yr,
    hs,
    hr,
    acc,
    xs_sem,
    xr_sem,
    ys_sem,
    yr_sem,
    hs_sem,
    hr_sem,
    out_sem,
):
    me = lax.axis_index("mom")
    band = lax.axis_index("space")
    up, down = lax.rem(band + 1, bands), lax.rem(band + bands - 1, bands)
    half = points // 2
    size = plane_rows * ROWS
    part = peers * ROWS
    block = 8
    order = sorted(range(1, peers), key=lambda o: abs(2 * o - peers))

    barrier = pltpu.get_barrier_semaphore()
    for o in range(1, peers):
        pl.semaphore_signal(
            barrier, inc=1, device_id={"mom": lax.rem(me + o, peers)}, device_id_type=pl.DeviceIdType.MESH
        )
    for side in (up, down):
        pl.semaphore_signal(barrier, inc=1, device_id={"space": side}, device_id_type=pl.DeviceIdType.MESH)
    pl.semaphore_wait(barrier, peers + 1)

    def rows_of(peer):
        return pl.ds(pl.multiple_of(peer * size, 8), size)

    def x_copy(c, o):
        peer = lax.rem(me + o, peers)
        return pltpu.make_async_remote_copy(
            src_ref=xs.at[c, rows_of(peer)],
            dst_ref=xr.at[c, rows_of(me)],
            send_sem=xs_sem.at[c, o],
            recv_sem=xr_sem.at[c, o],
            device_id={"mom": peer},
            device_id_type=pl.DeviceIdType.MESH,
        )

    def x_own(c):
        return pltpu.make_async_copy(xs.at[c, rows_of(me)], xr.at[c, rows_of(me)], xs_sem.at[c, 0])

    def y_place(c, last):
        return last_ref.at[rows_of(me)] if last else yr.at[c, rows_of(me)]

    def y_copy(c, o, last):
        peer = lax.rem(me + o, peers)
        return pltpu.make_async_remote_copy(
            src_ref=ys.at[c, rows_of(peer)],
            dst_ref=y_place(c, last),
            send_sem=ys_sem.at[c, o],
            recv_sem=yr_sem.at[c, o],
            device_id={"mom": peer},
            device_id_type=pl.DeviceIdType.MESH,
        )

    def y_own(c, last):
        return pltpu.make_async_copy(ys.at[c, rows_of(me)], y_place(c, last), ys_sem.at[c, 0])

    def side_copy(which, side):
        return pltpu.make_async_remote_copy(
            src_ref=hs.at[which],
            dst_ref=hr.at[which],
            send_sem=hs_sem.at[which],
            recv_sem=hr_sem.at[which],
            device_id={"space": side},
            device_id_type=pl.DeviceIdType.MESH,
        )

    def forward(c, carry):
        taken = pl.ds(pl.multiple_of(c * part, 16), part)

        def planes(g, inner):
            wh, wl = wh_ref[taken, :], wl_ref[taken, :]
            for a in range(block):
                k = g * block + a
                y = left_product(wh, wl, x_ref[k])
                for d in range(peers):
                    at = pl.multiple_of((d * plane_rows + k) * ROWS, 8)
                    xs[c, pl.ds(at, ROWS), :] = y[d * ROWS : (d + 1) * ROWS]
            return inner

        lax.fori_loop(0, plane_rows // block, planes, 0)
        for o in order:
            x_copy(c, o).start()
        x_own(c).start()
        return carry

    lax.fori_loop(0, chunks, forward, 0)

    lane = lax.broadcasted_iota(jnp.int32, (half, cells), 1)

    def pack(k, carry):
        x = x_ref[k]
        top, bottom = x[:half], x[half:]
        at = pl.ds(pl.multiple_of(k * half, 8), half)
        hs[0, at, :] = jnp.where(lane < cells // 2, pltpu.roll(top, cells // 2, 1), bottom)
        hs[1, at, :] = jnp.where(lane < cells // 2, top, pltpu.roll(bottom, cells // 2, 1))
        return carry

    lax.fori_loop(0, plane_rows, pack, 0)
    side_copy(0, up).start()
    side_copy(1, down).start()

    row = lax.broadcasted_iota(jnp.int32, (points, 2 * cells), 0)
    speed = (2 * row - (points - 1)).astype(F32) * (FRICTION / points)
    cell_row = lax.broadcasted_iota(jnp.int32, (points, cells), 0)
    signed = jnp.where(cell_row < half, cell_row, cell_row - points)
    squares = signed * signed
    exact = dict(precision=lax.Precision.HIGHEST, preferred_element_type=F32)
    scale = DAMPING / (half * half)

    def middle(c, last):
        for o in order:
            x_copy(c, o).wait_recv()
        x_own(c).wait()
        for i in range(PER):
            mode = me * (chunks * PER) + c * PER + i
            re = xr[c, pl.ds(2 * i, points, stride=ROWS), :]
            im = xr[c, pl.ds(2 * i + 1, points, stride=ROWS), :]
            x = jnp.concatenate([re, im], axis=1)
            pq = left_product(th_ref[...], tl_ref[...], x)
            pr, pi = pq[:points, :cells], pq[:points, cells:]
            qr, qi = pq[points:, :cells], pq[points:, cells:]
            s = jnp.dot(a_ref[...], b_ref[c * PER + i], **exact)
            d = scale * (squares + mode * mode).astype(F32)
            xre, xim = pr + qi, pi - qr
            ur = -d * xre - s * xim
            ui = s * xre - d * xim
            vr, vi = -ui, ur
            if i == 0:
                end = jnp.dot(a_ref[...], b_ref[chunks * PER], **exact)
                de = scale * (squares + half * half).astype(F32)
                real = mode == 0
                ur = jnp.where(real, s * qr - d * pr, ur)
                ui = jnp.where(real, end * qi - de * pi, ui)
                vr = jnp.where(real, -d * qr - s * pr, vr)
                vi = jnp.where(real, -de * qi - end * pi, vi)
            uv = jnp.concatenate(
                [jnp.concatenate([ur, ui], axis=1), jnp.concatenate([vr, vi], axis=1)], axis=0
            )
            y = left_product(ih_ref[...], il_ref[...], uv) + difference(speed * x, row, points)
            ys[c, pl.ds(2 * i, points, stride=ROWS), :] = y[:, :cells]
            ys[c, pl.ds(2 * i + 1, points, stride=ROWS), :] = y[:, cells:]
        for o in order:
            y_copy(c, o, last).start()
        y_own(c, last).start()

    def middle_step(c, carry):
        middle(c, False)
        return carry

    if chunks > 1:
        lax.fori_loop(0, chunks - 1, middle_step, 0)
    middle(chunks - 1, True)

    side_copy(0, up).wait_recv()
    side_copy(1, down).wait_recv()
    cell_speed = (2 * cell_row - (points - 1)).astype(F32) / points

    def advect(g, carry):
        for a in range(block):
            k = g * block + a
            x = x_ref[k]
            at = pl.ds(pl.multiple_of(k * half, 8), half)
            top = exact_product(x[:half], plus_ref[...])
            bottom = exact_product(x[half:], minus_ref[...])
            sides = exact_product(hr[0, at, :], lt_ref[...]) + exact_product(hr[1, at, :], rt_ref[...])
            rows = jnp.concatenate(
                [top[:, :cells] + sides[:, :cells], bottom[:, :cells] + sides[:, cells:]], 0
            )
            columns = jnp.concatenate([top[:, cells:], bottom[:, cells:]], 0)
            first = (2 * (me * plane_rows + k) - (points - 1)).astype(F32) * (1.0 / points)
            acc[k] = FRICTION * difference(cell_speed * x, cell_row, points) - (
                first * rows + cell_speed * columns
            ) * (1.0 / 60.0)
        return carry

    lax.fori_loop(0, plane_rows // block, advect, 0)

    def gather(c, carry):
        for o in order:
            y_copy(c, o, False).wait_recv()
        y_own(c, False).wait()

        def planes(g, inner):
            for a in range(block):
                k = g * block + a
                y = jnp.concatenate(
                    [
                        yr[c, pl.ds(pl.multiple_of((d * plane_rows + k) * ROWS, 8), ROWS), :]
                        for d in range(peers)
                    ],
                    axis=0,
                )
                acc[k] += left_product(bh_ref[c], bl_ref[c], y)
            return inner

        lax.fori_loop(0, plane_rows // block, planes, 0)
        return carry

    if chunks > 1:
        lax.fori_loop(0, chunks - 1, gather, 0)
    out = pltpu.make_async_copy(acc, out_ref, out_sem)
    out.start()

    def sent(c, carry):
        for o in order:
            x_copy(c, o).wait_send()
        return carry

    def sent_back(c, carry):
        for o in order:
            y_copy(c, o, False).wait_send()
        return carry

    lax.fori_loop(0, chunks, sent, 0)
    if chunks > 1:
        lax.fori_loop(0, chunks - 1, sent_back, 0)
    side_copy(0, up).wait_send()
    side_copy(1, down).wait_send()
    out.wait()
    for o in order:
        y_copy(chunks - 1, o, True).wait()
    y_own(chunks - 1, True).wait()


def back_kernel(peers, block, base_ref, wh_ref, wl_ref, y_ref, o_ref):
    for a in range(block):
        y = jnp.concatenate([y_ref[d, a] for d in range(peers)], axis=0)
        o_ref[a] = base_ref[a] + left_product(wh_ref[...], wl_ref[...], y)


def whole(shape):
    return pl.BlockSpec(shape, lambda *_: (0,) * len(shape))


def params(mib=48):
    return pltpu.CompilerParams(vmem_limit_bytes=mib * 2**20)


def cost(flops, size):
    return pl.CostEstimate(flops=int(flops), bytes_accessed=int(size), transcendentals=0)


def local(density, mode_waves, mode_amplitudes, mode_phases):
    plane_rows, points, cells = density.shape
    rows_dev = cells // NY
    peers = lax.axis_size("mom")
    bands = lax.axis_size("space")
    total_rows = rows_dev * bands
    mom = lax.axis_index("mom")
    space = lax.axis_index("space")
    per_peer = points // 2 // peers
    chunks = per_peer // PER
    block = 8
    steps = plane_rows // block
    half = points // 2
    size = plane_rows * points * cells * 4

    forward, back = second_tables(points, peers)
    part = peers * ROWS
    wh, wl = halves(forward)
    bh, bl = halves(np.stack([back[:, c * part : (c + 1) * part] for c in range(chunks)]))
    first, inverse = first_tables(points)
    th, tl = halves(first)
    ih, il = halves(inverse)

    index = jnp.arange(points, dtype=jnp.int32)
    signed = jnp.where(index < half, index, index - points)
    unit = np.float32(np.pi / points)
    a_angle = unit * (mode_waves[None, :, 0] * signed[:, None] % (2 * points)).astype(F32)
    a_sine = jnp.where(index[:, None] == half, 0.0, jnp.sin(a_angle))
    a_table = jnp.concatenate([a_sine, jnp.cos(a_angle)], axis=1)
    cell = jnp.arange(cells, dtype=jnp.int32)
    turn_rows = mode_waves[:, 0:1] * (space * rows_dev + cell // NY)[None, :] % total_rows
    turn_columns = mode_waves[:, 1:2] * (cell % NY)[None, :] % NY
    angles = (
        2.0 * np.pi * (turn_rows.astype(F32) / total_rows + turn_columns.astype(F32) / NY)
        + mode_phases[:, None]
    )
    cell_factor = mode_amplitudes[:, None] * jnp.sin(angles)

    def mode_factors(modes):
        b_angle = unit * (mode_waves[None, :, 1] * modes[:, None] % (2 * points)).astype(F32)
        waves = jnp.concatenate([jnp.cos(b_angle), jnp.sin(b_angle)], axis=1)
        return waves[:, :, None] * jnp.concatenate([cell_factor, cell_factor], axis=0)[None]

    modes = mom * per_peer + jnp.arange(per_peer, dtype=jnp.int32)
    b_table = mode_factors(jnp.concatenate([modes, jnp.full((1,), -half, jnp.int32)]))

    positive = mom * plane_rows >= half
    own_m, left_m, right_m = row_tables(cells, MINUS)
    own_p, left_p, right_p = row_tables(cells, PLUS)

    def chosen(minus, plus):
        return jnp.where(positive, jnp.asarray(minus, BF16), jnp.asarray(plus, BF16))

    def beside(columns):
        return chosen(np.concatenate([own_m, columns], 1), np.concatenate([own_p, columns], 1))

    vm = pl.BlockSpec(memory_space=pltpu.VMEM)
    anywhere = pl.BlockSpec(memory_space=pl.ANY)
    message_rows = peers * plane_rows * ROWS
    chunked = pltpu.VMEM((chunks, message_rows, cells), F32)
    sides = pltpu.VMEM((2, plane_rows * half, cells), F32)
    flags = pltpu.SemaphoreType.DMA((chunks, peers))
    pair = pltpu.SemaphoreType.DMA((2,))
    base, last = pl.pallas_call(
        functools.partial(exchange_kernel, peers, bands, chunks, plane_rows, points, cells),
        out_shape=[
            jax.ShapeDtypeStruct(density.shape, F32),
            jax.ShapeDtypeStruct((message_rows, cells), F32),
        ],
        in_specs=[vm] * 15,
        out_specs=[anywhere] * 2,
        scratch_shapes=[chunked] * 4
        + [sides] * 2
        + [pltpu.VMEM(density.shape, F32)]
        + [flags] * 4
        + [pair] * 2
        + [pltpu.SemaphoreType.DMA],
        compiler_params=pltpu.CompilerParams(
            vmem_limit_bytes=56 * 2**20, collective_id=0, has_side_effects=True
        ),
        cost_estimate=cost(3 * 3.2e9, 3 * size),
        name="exchange",
    )(
        density,
        wh,
        wl,
        th,
        tl,
        ih,
        il,
        a_table,
        b_table,
        beside(column_table(cells, PLUS)),
        beside(column_table(cells, MINUS)),
        chosen(left_m, left_p),
        chosen(right_m, right_p),
        bh,
        bl,
    )
    plane = lambda g: (g, 0, 0)
    return pl.pallas_call(
        functools.partial(back_kernel, peers, block),
        grid=(steps,),
        out_shape=jax.ShapeDtypeStruct(density.shape, F32),
        in_specs=[
            pl.BlockSpec((block, points, cells), plane),
            whole(bh.shape[1:]),
            whole(bl.shape[1:]),
            pl.BlockSpec((peers, block, ROWS, cells), lambda g: (0, g, 0, 0)),
        ],
        out_specs=pl.BlockSpec((block, points, cells), plane),
        compiler_params=params(),
        cost_estimate=cost(6 * plane_rows * points * part * cells, 3 * size),
        name="second_inverse",
    )(base, bh[-1], bl[-1], last.reshape(peers, plane_rows, ROWS, cells))


def solution(mesh):
    return jax.shard_map(
        local,
        mesh=mesh,
        in_specs=(P("mom", None, "space"), P(), P(), P()),
        out_specs=P("mom", None, "space"),
        check_vma=False,
    )
```

time: 312 us -> 204 us (0.65)
  the two profiles are of different devices: /device:TPU:0 before, /device:TPU:9 now
where the time goes in v2:
time: 204 us
  Pallas kernels  194 us (95%)
  other arithmetic  5.23 us (3%)
  local copies, waits for them, and re-layouts  4.92 us (2%)
    pallas_call x1, Pallas kernels, local(): pl.pallas_call(functools.partial(exchange_kernel, peers, bands, chunks, p...  190 us

profile of v2, /device:TPU:9, one launch (start us, length us, event | category | flops | bytes accessed | tf_op | source)
XLA Modules:
  0.0 203.9 jit_solution(11963816926139694873)
XLA Ops:
  0.0 0.1 pad_add_fusion
  0.1 0.8 slice_bitcast_fusion
  0.9 0.8 fusion.12
  1.7 0.1 fusion.19
  1.8 0.1 pad_maximum_fusion.2
  1.9 0.2 sine_select_fusion
  2.1 0.7 copy.21.a_ref
  2.8 1.6 broadcast_select_fusion.2
  4.4 1.6 broadcast_select_fusion
  5.9 0.8 broadcast_multiply_fusion.b_ref
  6.8 0.0 copy-start.2
  6.8 0.0 copy-start.3
  6.8 190.0 %exchange.1 = (f32[32,256,128]{2,1,0:T(8,128)}, f32[2048,128]{1,0:T(8,128)}) custom-call(f32[32,256,128]{2,1,0:T(8,128)} %x_ref.1, bf16[256,256]{1,0:T(8,128)(2,1)} %constant.136.clone.wh_ref, bf16[256,256]{1,0:T(8,128)(2,1)} %constant.137.clone.wl_ref, bf16[512,256]{1,0:T(8,128)(2,1)} %constant.140.clone.th_ref, bf16[512,256]{1,0:T(8,128)(2,1)} %constant.141.clone.tl_ref, ...), custom_call_target="tpu_custom_call" | custom-call | flops 9600000000 | bytes 12582912 | tf_op jit(solution)/shard_map/exchange/pallas_call | solution.py:455
  196.8 0.0 copy-done.2
  196.8 0.0 copy-done.3
  196.8 0.0 copy-start
  196.8 2.2 %copy-done = f32[32,256,128]{2,1,0:T(8,128)S(1)} copy-done((f32[32,256,128]{2,1,0:T(8,128)S(1)}, f32[32,256,128]{2,1,0:T(8,128)}, u32[]{:S(2)}) %copy-start) | copy-done | bytes 4194328
  199.0 0.0 copy-start.1
  199.0 1.2 copy-done.1
  200.2 3.7 %second_inverse.1 = f32[32,256,128]{2,1,0:T(8,128)} custom-call(f32[32,256,128]{2,1,0:T(8,128)S(1)} %copy-done, bf16[256,64]{1,0:T(8,128)(2,1)S(1)} %copy-done.3, bf16[256,64]{1,0:T(8,128)(2,1)S(1)} %copy-done.2, f32[8,32,8,128]{3,2,1,0:T(8,128)S(1)} %bitcast.5), custom_call_target="tpu_custom_call" | custom-call | flops 402653184 | bytes 12582912 | tf_op jit(solution)/shard_map/second_inverse/pallas_call | solution.py:492
  (6 shorter events, 0.0 us)
Async XLA Ops:
  6.8 190.0 %copy-start.2 = (bf16[256,64]{1,0:T(8,128)(2,1)S(1)}, bf16[256,64]{1,0:T(8,128)(2,1)}, u32[]{:S(2)}) copy-start(bf16[256,64]{1,0:T(8,128)(2,1)} %constant.155.wl_ref) | copy-start | bytes 98308
  6.8 190.1 %copy-start.3 = (bf16[256,64]{1,0:T(8,128)(2,1)S(1)}, bf16[256,64]{1,0:T(8,128)(2,1)}, u32[]{:S(2)}) copy-start(bf16[256,64]{1,0:T(8,128)(2,1)} %constant.153.wh_ref) | copy-start | bytes 98308
  196.8 2.2 %copy-start = (f32[32,256,128]{2,1,0:T(8,128)S(1)}, f32[32,256,128]{2,1,0:T(8,128)}, u32[]{:S(2)}) copy-start(f32[32,256,128]{2,1,0:T(8,128)} %get-tuple-element.7.base_ref) | copy-start | bytes 12582916
  199.0 1.2 copy-start.1

commit v3 on v2

--- a/solution.py
+++ b/solution.py
@@ -119,15 +119,16 @@
     plane_rows,
     points,
     cells,
-    x_ref,
+    source_ref,
     wh_ref,
     wl_ref,
     th_ref,
     tl_ref,
     ih_ref,
     il_ref,
-    a_ref,
-    b_ref,
+    waves_ref,
+    amp_ref,
+    phase_ref,
     plus_ref,
     minus_ref,
     lt_ref,
@@ -143,6 +144,9 @@
     hs,
     hr,
     acc,
+    x_ref,
+    a_ref,
+    cf_ref,
     xs_sem,
     xr_sem,
     ys_sem,
@@ -150,6 +154,7 @@
     hs_sem,
     hr_sem,
     out_sem,
+    in_sem,
 ):
     me = lax.axis_index("mom")
     band = lax.axis_index("space")
@@ -158,7 +163,19 @@
     size = plane_rows * ROWS
     part = peers * ROWS
     block = 8
-    order = sorted(range(1, peers), key=lambda o: abs(2 * o - peers))
+    groups = plane_rows // block
+    side = peers // 2
+    mine = me // side * side
+    far = side - mine
+    order = [far + lax.rem(me + j, side) for j in range(side)]
+    order += [mine + lax.rem(me + j, side) for j in range(1, side)]
+
+    def load(g):
+        planes = pl.ds(pl.multiple_of(g * block, block), block)
+        return pltpu.make_async_copy(source_ref.at[planes], x_ref.at[planes], in_sem.at[g])
+
+    for g in range(groups):
+        load(g).start()
 
     barrier = pltpu.get_barrier_semaphore()
     for o in range(1, peers):
@@ -167,41 +184,38 @@
         )
     for side in (up, down):
         pl.semaphore_signal(barrier, inc=1, device_id={"space": side}, device_id_type=pl.DeviceIdType.MESH)
-    pl.semaphore_wait(barrier, peers + 1)
 
     def rows_of(peer):
         return pl.ds(pl.multiple_of(peer * size, 8), size)
 
-    def x_copy(c, o):
-        peer = lax.rem(me + o, peers)
+    def x_copy(c, peer, source=me):
         return pltpu.make_async_remote_copy(
             src_ref=xs.at[c, rows_of(peer)],
             dst_ref=xr.at[c, rows_of(me)],
-            send_sem=xs_sem.at[c, o],
-            recv_sem=xr_sem.at[c, o],
+            send_sem=xs_sem.at[c, peer],
+            recv_sem=xr_sem.at[c, source],
             device_id={"mom": peer},
             device_id_type=pl.DeviceIdType.MESH,
         )
 
     def x_own(c):
-        return pltpu.make_async_copy(xs.at[c, rows_of(me)], xr.at[c, rows_of(me)], xs_sem.at[c, 0])
+        return pltpu.make_async_copy(xs.at[c, rows_of(me)], xr.at[c, rows_of(me)], xs_sem.at[c, me])
 
     def y_place(c, last):
         return last_ref.at[rows_of(me)] if last else yr.at[c, rows_of(me)]
 
-    def y_copy(c, o, last):
-        peer = lax.rem(me + o, peers)
+    def y_copy(c, peer, last, source=me):
         return pltpu.make_async_remote_copy(
             src_ref=ys.at[c, rows_of(peer)],
             dst_ref=y_place(c, last),
-            send_sem=ys_sem.at[c, o],
-            recv_sem=yr_sem.at[c, o],
+            send_sem=ys_sem.at[c, peer],
+            recv_sem=yr_sem.at[c, source],
             device_id={"mom": peer},
             device_id_type=pl.DeviceIdType.MESH,
         )
 
     def y_own(c, last):
-        return pltpu.make_async_copy(ys.at[c, rows_of(me)], y_place(c, last), ys_sem.at[c, 0])
+        return pltpu.make_async_copy(ys.at[c, rows_of(me)], y_place(c, last), ys_sem.at[c, me])
 
     def side_copy(which, side):
         return pltpu.make_async_remote_copy(
@@ -213,10 +227,12 @@
             device_id_type=pl.DeviceIdType.MESH,
         )
 
-    def forward(c, carry):
+    def transform(c, loading):
         taken = pl.ds(pl.multiple_of(c * part, 16), part)
 
         def planes(g, inner):
+            if loading:
+                load(g).wait()
             wh, wl = wh_ref[taken, :], wl_ref[taken, :]
             for a in range(block):
                 k = g * block + a
@@ -226,13 +242,23 @@
                     xs[c, pl.ds(at, ROWS), :] = y[d * ROWS : (d + 1) * ROWS]
             return inner
 
-        lax.fori_loop(0, plane_rows // block, planes, 0)
+        lax.fori_loop(0, groups, planes, 0)
+
+    def send(c):
         for o in order:
             x_copy(c, o).start()
         x_own(c).start()
-        return carry
-
-    lax.fori_loop(0, chunks, forward, 0)
+
+    def forward(c, carry):
+        transform(c, False)
+        send(c)
+        return carry
+
+    transform(0, True)
+    pl.semaphore_wait(barrier, peers + 1)
+    send(0)
+    if chunks > 1:
+        lax.fori_loop(1, chunks, forward, 0)
 
     lane = lax.broadcasted_iota(jnp.int32, (half, cells), 1)
 
@@ -256,9 +282,46 @@
     exact = dict(precision=lax.Precision.HIGHEST, preferred_element_type=F32)
     scale = DAMPING / (half * half)
 
+
+    modes = waves_ref.shape[0]
+    waves = waves_ref[...].astype(F32)
+    w_row, w_column = waves[:, 0:1], waves[:, 1:2]
+    eye = lax.broadcasted_iota(jnp.int32, (modes, modes), 0) == lax.broadcasted_iota(
+        jnp.int32, (modes, modes), 1
+    )
+
+    def upright(value):
+        return jnp.sum(jnp.where(eye, jnp.broadcast_to(value, (modes, modes)), 0.0), axis=1, keepdims=True)
+
+    def turned(value, period):
+        return value - period * jnp.floor(value / period)
+
+    unit = np.float32(np.pi / points)
+    freq = lax.broadcasted_iota(jnp.int32, (modes, points), 1)
+    freq_signed = jnp.where(freq < half, freq, freq - points).astype(F32)
+    a_angle = unit * turned(w_row * freq_signed, 2.0 * points)
+    a_ref[:modes] = jnp.where(freq == half, 0.0, jnp.sin(a_angle))
+    a_ref[modes:] = jnp.cos(a_angle)
+    rows_dev = cells // NY
+    cell = lax.broadcasted_iota(jnp.int32, (modes, cells), 1).astype(F32)
+    cell_line = jnp.floor(cell / NY)
+    cell_column = cell - NY * cell_line
+    cell_line = cell_line + (band * rows_dev).astype(F32)
+    total_rows = float(rows_dev * bands)
+    angles = (
+        2.0 * np.pi * (turned(w_row * cell_line, total_rows) / total_rows + turned(w_column * cell_column, float(NY)) / NY)
+        + upright(phase_ref[...])
+    )
+    cf_ref[...] = upright(amp_ref[...]) * jnp.sin(angles)
+
+    def symbol(mode):
+        b_angle = unit * turned(w_column * jnp.full((modes, cells), mode, jnp.int32).astype(F32), 2.0 * points)
+        factor = jnp.concatenate([jnp.cos(b_angle) * cf_ref[...], jnp.sin(b_angle) * cf_ref[...]], axis=0)
+        return lax.dot_general(a_ref[...], factor, (((0,), (0,)), ((), ())), **exact)
+
     def middle(c, last):
         for o in order:
-            x_copy(c, o).wait_recv()
+            x_copy(c, o, o).wait_recv()
         x_own(c).wait()
         for i in range(PER):
             mode = me * (chunks * PER) + c * PER + i
@@ -268,14 +331,14 @@
             pq = left_product(th_ref[...], tl_ref[...], x)
             pr, pi = pq[:points, :cells], pq[:points, cells:]
             qr, qi = pq[points:, :cells], pq[points:, cells:]
-            s = jnp.dot(a_ref[...], b_ref[c * PER + i], **exact)
+            s = symbol(mode)
             d = scale * (squares + mode * mode).astype(F32)
             xre, xim = pr + qi, pi - qr
             ur = -d * xre - s * xim
             ui = s * xre - d * xim
             vr, vi = -ui, ur
             if i == 0:
-                end = jnp.dot(a_ref[...], b_ref[chunks * PER], **exact)
+                end = symbol(-half)
                 de = scale * (squares + half * half).astype(F32)
                 real = mode == 0
                 ur = jnp.where(real, s * qr - d * pr, ur)
@@ -302,6 +365,7 @@
 
     side_copy(0, up).wait_recv()
     side_copy(1, down).wait_recv()
+    stencil = me * plane_rows // half
     cell_speed = (2 * cell_row - (points - 1)).astype(F32) / points
 
     def advect(g, carry):
@@ -309,9 +373,9 @@
             k = g * block + a
             x = x_ref[k]
             at = pl.ds(pl.multiple_of(k * half, 8), half)
-            top = exact_product(x[:half], plus_ref[...])
-            bottom = exact_product(x[half:], minus_ref[...])
-            sides = exact_product(hr[0, at, :], lt_ref[...]) + exact_product(hr[1, at, :], rt_ref[...])
+            top = exact_product(x[:half], plus_ref[stencil])
+            bottom = exact_product(x[half:], minus_ref[stencil])
+            sides = exact_product(hr[0, at, :], lt_ref[stencil]) + exact_product(hr[1, at, :], rt_ref[stencil])
             rows = jnp.concatenate(
                 [top[:, :cells] + sides[:, :cells], bottom[:, :cells] + sides[:, cells:]], 0
             )
@@ -326,7 +390,7 @@
 
     def gather(c, carry):
         for o in order:
-            y_copy(c, o, False).wait_recv()
+            y_copy(c, o, False, o).wait_recv()
         y_own(c, False).wait()
 
         def planes(g, inner):
@@ -367,7 +431,9 @@
     side_copy(1, down).wait_send()
     out.wait()
     for o in order:
-        y_copy(chunks - 1, o, True).wait()
+        y_copy(chunks - 1, o, True).wait_send()
+    for o in order:
+        y_copy(chunks - 1, o, True, o).wait_recv()
     y_own(chunks - 1, True).wait()
 
 
@@ -391,12 +457,8 @@
 
 def local(density, mode_waves, mode_amplitudes, mode_phases):
     plane_rows, points, cells = density.shape
-    rows_dev = cells // NY
     peers = lax.axis_size("mom")
     bands = lax.axis_size("space")
-    total_rows = rows_dev * bands
-    mom = lax.axis_index("mom")
-    space = lax.axis_index("space")
     per_peer = points // 2 // peers
     chunks = per_peer // PER
     block = 8
@@ -412,35 +474,11 @@
     th, tl = halves(first)
     ih, il = halves(inverse)
 
-    index = jnp.arange(points, dtype=jnp.int32)
-    signed = jnp.where(index < half, index, index - points)
-    unit = np.float32(np.pi / points)
-    a_angle = unit * (mode_waves[None, :, 0] * signed[:, None] % (2 * points)).astype(F32)
-    a_sine = jnp.where(index[:, None] == half, 0.0, jnp.sin(a_angle))
-    a_table = jnp.concatenate([a_sine, jnp.cos(a_angle)], axis=1)
-    cell = jnp.arange(cells, dtype=jnp.int32)
-    turn_rows = mode_waves[:, 0:1] * (space * rows_dev + cell // NY)[None, :] % total_rows
-    turn_columns = mode_waves[:, 1:2] * (cell % NY)[None, :] % NY
-    angles = (
-        2.0 * np.pi * (turn_rows.astype(F32) / total_rows + turn_columns.astype(F32) / NY)
-        + mode_phases[:, None]
-    )
-    cell_factor = mode_amplitudes[:, None] * jnp.sin(angles)
-
-    def mode_factors(modes):
-        b_angle = unit * (mode_waves[None, :, 1] * modes[:, None] % (2 * points)).astype(F32)
-        waves = jnp.concatenate([jnp.cos(b_angle), jnp.sin(b_angle)], axis=1)
-        return waves[:, :, None] * jnp.concatenate([cell_factor, cell_factor], axis=0)[None]
-
-    modes = mom * per_peer + jnp.arange(per_peer, dtype=jnp.int32)
-    b_table = mode_factors(jnp.concatenate([modes, jnp.full((1,), -half, jnp.int32)]))
-
-    positive = mom * plane_rows >= half
     own_m, left_m, right_m = row_tables(cells, MINUS)
     own_p, left_p, right_p = row_tables(cells, PLUS)
 
     def chosen(minus, plus):
-        return jnp.where(positive, jnp.asarray(minus, BF16), jnp.asarray(plus, BF16))
+        return jnp.asarray(np.stack([plus, minus]).astype(ml_dtypes.bfloat16))
 
     def beside(columns):
         return chosen(np.concatenate([own_m, columns], 1), np.concatenate([own_p, columns], 1))
@@ -458,14 +496,16 @@
             jax.ShapeDtypeStruct(density.shape, F32),
             jax.ShapeDtypeStruct((message_rows, cells), F32),
         ],
-        in_specs=[vm] * 15,
+        in_specs=[anywhere] + [vm] * 15,
         out_specs=[anywhere] * 2,
         scratch_shapes=[chunked] * 4
         + [sides] * 2
-        + [pltpu.VMEM(density.shape, F32)]
+        + [pltpu.VMEM(density.shape, F32)] * 2
+        + [pltpu.VMEM((2 * mode_waves.shape[0], points), F32)]
+        + [pltpu.VMEM((mode_waves.shape[0], cells), F32)]
         + [flags] * 4
         + [pair] * 2
-        + [pltpu.SemaphoreType.DMA],
+        + [pltpu.SemaphoreType.DMA, pltpu.SemaphoreType.DMA((steps,))],
         compiler_params=pltpu.CompilerParams(
             vmem_limit_bytes=56 * 2**20, collective_id=0, has_side_effects=True
         ),
@@ -479,8 +519,9 @@
         tl,
         ih,
         il,
-        a_table,
-        b_table,
+        mode_waves,
+        mode_amplitudes.reshape(1, -1),
+        mode_phases.reshape(1, -1),
         beside(column_table(cells, PLUS)),
         beside(column_table(cells, MINUS)),
         chosen(left_m, left_p),
@@ -500,7 +541,7 @@
             pl.BlockSpec((peers, block, ROWS, cells), lambda g: (0, g, 0, 0)),
         ],
         out_specs=pl.BlockSpec((block, points, cells), plane),
-        compiler_params=params(),
+        compiler_params=params(60),
         cost_estimate=cost(6 * plane_rows * points * part * cells, 3 * size),
         name="second_inverse",
     )(base, bh[-1], bl[-1], last.reshape(peers, plane_rows, ROWS, cells))

time: 204 us -> 197 us (0.966)
  the two profiles are of different devices: /device:TPU:9 before, /device:TPU:0 now
where the time goes in v3:
time: 197 us
  Pallas kernels  196 us (99%)
    pallas_call x1, Pallas kernels, local(): pl.pallas_call(functools.partial(exchange_kernel, peers, bands, chunks, p...  190 us
    pallas_call x1, Pallas kernels, local(): pl.pallas_call(functools.partial(back_kernel, peers, block), grid=(steps,...  5.97 us

profile of v3, /device:TPU:0, one launch (start us, length us, event | category | flops | bytes accessed | tf_op | source)
XLA Modules:
  0.0 196.9 jit_solution(590999355194725000)
XLA Ops:
  0.0 1.4 copy.17.waves_ref
  1.4 189.6 %exchange.1 = (f32[32,256,128]{2,1,0:T(8,128)}, f32[2048,128]{1,0:T(8,128)}) custom-call(f32[32,256,128]{2,1,0:T(8,128)} %source_ref.1, bf16[256,256]{1,0:T(8,128)(2,1)} %constant.24.clone.wh_ref, bf16[256,256]{1,0:T(8,128)(2,1)} %constant.25.clone.wl_ref, bf16[512,256]{1,0:T(8,128)(2,1)} %constant.28.clone.th_ref, bf16[512,256]{1,0:T(8,128)(2,1)} %constant.29.clone.tl_ref, ...), custom_call_target="tpu_custom_call" | custom-call | flops 9600000000 | bytes 12582912 | tf_op jit(solution)/shard_map/exchange/pallas_call | solution.py:493
  190.9 6.0 %second_inverse.1 = f32[32,256,128]{2,1,0:T(8,128)} custom-call(f32[32,256,128]{2,1,0:T(8,128)} %get-tuple-element.7.base_ref, bf16[256,64]{1,0:T(8,128)(2,1)} %constant.37.wh_ref, bf16[256,64]{1,0:T(8,128)(2,1)} %constant.39.wl_ref, f32[8,32,8,128]{3,2,1,0:T(8,128)} %bitcast.3), custom_call_target="tpu_custom_call" | custom-call | flops 402653184 | bytes 12582912 | tf_op jit(solution)/shard_map/second_inverse/pallas_call | solution.py:533

commit v4 on v3

--- a/solution.py
+++ b/solution.py
@@ -23,7 +23,7 @@
 def halves(table):
     high = table.astype(ml_dtypes.bfloat16)
     low = (table - high.astype(np.float64)).astype(ml_dtypes.bfloat16)
-    return jnp.asarray(high), jnp.asarray(low)
+    return high, low
 
 
 def mode_order(points, peers):
@@ -104,6 +104,11 @@
 def exact_product(value, table):
     vh, vl = split(value)
     return mm(vh, table) + mm(vl, table)
+
+
+def stacked_product(table, value):
+    vh, vl = split(value)
+    return mm(table, jnp.concatenate([vh, vh, vl], axis=0))
 
 
 def difference(weighted, row, points):
@@ -133,8 +138,7 @@
     minus_ref,
     lt_ref,
     rt_ref,
-    bh_ref,
-    bl_ref,
+    bs_ref,
     out_ref,
     last_ref,
     xs,
@@ -234,12 +238,13 @@
             if loading:
                 load(g).wait()
             wh, wl = wh_ref[taken, :], wl_ref[taken, :]
-            for a in range(block):
+            for a in range(0, block, 2):
                 k = g * block + a
-                y = left_product(wh, wl, x_ref[k])
+                y = left_product(wh, wl, jnp.concatenate([x_ref[k], x_ref[k + 1]], axis=1))
                 for d in range(peers):
                     at = pl.multiple_of((d * plane_rows + k) * ROWS, 8)
-                    xs[c, pl.ds(at, ROWS), :] = y[d * ROWS : (d + 1) * ROWS]
+                    xs[c, pl.ds(at, ROWS), :] = y[d * ROWS : (d + 1) * ROWS, :cells]
+                    xs[c, pl.ds(at + ROWS, ROWS), :] = y[d * ROWS : (d + 1) * ROWS, cells:]
             return inner
 
         lax.fori_loop(0, groups, planes, 0)
@@ -283,9 +288,8 @@
     scale = DAMPING / (half * half)
 
 
-    modes = waves_ref.shape[0]
+    modes = waves_ref.shape[1]
     waves = waves_ref[...].astype(F32)
-    w_row, w_column = waves[:, 0:1], waves[:, 1:2]
     eye = lax.broadcasted_iota(jnp.int32, (modes, modes), 0) == lax.broadcasted_iota(
         jnp.int32, (modes, modes), 1
     )
@@ -296,6 +300,7 @@
     def turned(value, period):
         return value - period * jnp.floor(value / period)
 
+    w_row, w_column = upright(waves[0:1]), upright(waves[1:2])
     unit = np.float32(np.pi / points)
     freq = lax.broadcasted_iota(jnp.int32, (modes, points), 1)
     freq_signed = jnp.where(freq < half, freq, freq - points).astype(F32)
@@ -394,16 +399,21 @@
         y_own(c, False).wait()
 
         def planes(g, inner):
-            for a in range(block):
+            for a in range(0, block, 2):
                 k = g * block + a
-                y = jnp.concatenate(
-                    [
-                        yr[c, pl.ds(pl.multiple_of((d * plane_rows + k) * ROWS, 8), ROWS), :]
-                        for d in range(peers)
-                    ],
-                    axis=0,
-                )
-                acc[k] += left_product(bh_ref[c], bl_ref[c], y)
+                y = [
+                    jnp.concatenate(
+                        [
+                            yr[c, pl.ds(pl.multiple_of((d * plane_rows + k + b) * ROWS, 8), ROWS), :]
+                            for d in range(peers)
+                        ],
+                        axis=0,
+                    )
+                    for b in range(2)
+                ]
+                product = stacked_product(bs_ref[c], jnp.concatenate(y, axis=1))
+                acc[k] += product[:, :cells]
+                acc[k + 1] += product[:, cells:]
             return inner
 
         lax.fori_loop(0, plane_rows // block, planes, 0)
@@ -437,10 +447,12 @@
     y_own(chunks - 1, True).wait()
 
 
-def back_kernel(peers, block, base_ref, wh_ref, wl_ref, y_ref, o_ref):
-    for a in range(block):
-        y = jnp.concatenate([y_ref[d, a] for d in range(peers)], axis=0)
-        o_ref[a] = base_ref[a] + left_product(wh_ref[...], wl_ref[...], y)
+def back_kernel(peers, cells, block, base_ref, table_ref, y_ref, o_ref):
+    for a in range(0, block, 2):
+        y = [jnp.concatenate([y_ref[d, a + b] for d in range(peers)], axis=0) for b in range(2)]
+        product = stacked_product(table_ref[...], jnp.concatenate(y, axis=1))
+        o_ref[a] = base_ref[a] + product[:, :cells]
+        o_ref[a + 1] = base_ref[a + 1] + product[:, cells:]
 
 
 def whole(shape):
@@ -470,6 +482,8 @@
     part = peers * ROWS
     wh, wl = halves(forward)
     bh, bl = halves(np.stack([back[:, c * part : (c + 1) * part] for c in range(chunks)]))
+    bs = jnp.asarray(np.concatenate([bh, bl, bh], axis=2))
+    last_table = jnp.asarray(np.concatenate([bh[-1], bl[-1], bh[-1]], axis=1))
     first, inverse = first_tables(points)
     th, tl = halves(first)
     ih, il = halves(inverse)
@@ -496,7 +510,7 @@
             jax.ShapeDtypeStruct(density.shape, F32),
             jax.ShapeDtypeStruct((message_rows, cells), F32),
         ],
-        in_specs=[anywhere] + [vm] * 15,
+        in_specs=[anywhere] + [vm] * 14,
         out_specs=[anywhere] * 2,
         scratch_shapes=[chunked] * 4
         + [sides] * 2
@@ -519,32 +533,30 @@
         tl,
         ih,
         il,
-        mode_waves,
+        mode_waves.T,
         mode_amplitudes.reshape(1, -1),
         mode_phases.reshape(1, -1),
         beside(column_table(cells, PLUS)),
         beside(column_table(cells, MINUS)),
         chosen(left_m, left_p),
         chosen(right_m, right_p),
-        bh,
-        bl,
+        bs,
     )
     plane = lambda g: (g, 0, 0)
     return pl.pallas_call(
-        functools.partial(back_kernel, peers, block),
+        functools.partial(back_kernel, peers, cells, block),
         grid=(steps,),
         out_shape=jax.ShapeDtypeStruct(density.shape, F32),
         in_specs=[
             pl.BlockSpec((block, points, cells), plane),
-            whole(bh.shape[1:]),
-            whole(bl.shape[1:]),
+            whole(bs.shape[1:]),
             pl.BlockSpec((peers, block, ROWS, cells), lambda g: (0, g, 0, 0)),
         ],
         out_specs=pl.BlockSpec((block, points, cells), plane),
         compiler_params=params(60),
         cost_estimate=cost(6 * plane_rows * points * part * cells, 3 * size),
         name="second_inverse",
-    )(base, bh[-1], bl[-1], last.reshape(peers, plane_rows, ROWS, cells))
+    )(base, last_table, last.reshape(peers, plane_rows, ROWS, cells))
 
 
 def solution(mesh):

time: 197 us -> 195 us (0.990)
  no operation moved by 1% of the time
where the time goes in v4:
time: 195 us
  Pallas kernels  195 us (100%)
    pallas_call x1, Pallas kernels, local(): pl.pallas_call(functools.partial(exchange_kernel, peers, bands, chunks, p...  190 us
    pallas_call x1, Pallas kernels, local(): pl.pallas_call(functools.partial(back_kernel, peers, cells, block), grid=...  5.34 us

profile of v4, /device:TPU:0, one launch (start us, length us, event | category | flops | bytes accessed | tf_op | source)
XLA Modules:
  0.0 195.0 jit_solution(3994972769919097741)
XLA Ops:
  0.0 189.7 %exchange.1 = (f32[32,256,128]{2,1,0:T(8,128)}, f32[2048,128]{1,0:T(8,128)}) custom-call(f32[32,256,128]{2,1,0:T(8,128)} %source_ref.1, bf16[256,256]{1,0:T(8,128)(2,1)} %constant.30.clone.wh_ref, bf16[256,256]{1,0:T(8,128)(2,1)} %constant.31.clone.wl_ref, bf16[512,256]{1,0:T(8,128)(2,1)} %constant.32.clone.th_ref, bf16[512,256]{1,0:T(8,128)(2,1)} %constant.33.clone.tl_ref, ...), custom_call_target="tpu_custom_call" | custom-call | flops 9600000000 | bytes 12582912 | tf_op jit(solution)/shard_map/exchange/pallas_call | solution.py:507
  189.7 5.3 %second_inverse.1 = f32[32,256,128]{2,1,0:T(8,128)} custom-call(f32[32,256,128]{2,1,0:T(8,128)} %get-tuple-element.7.base_ref, bf16[256,192]{1,0:T(8,128)(2,1)} %constant.25.clone.table_ref, f32[8,32,8,128]{3,2,1,0:T(8,128)} %bitcast.4), custom_call_target="tpu_custom_call" | custom-call | flops 402653184 | bytes 12582912 | tf_op jit(solution)/shard_map/second_inverse/pallas_call | solution.py:546
